TPU v7x, 32 devices: a whole 2x2x4 slice. The times are simulated.
32 devices in a mesh: dp: 8 (over y, x, core), freq: 4 (over z).
Axes of the slice: x: 2, y: 2, z: 4, core: 2. Of those that a mesh axis runs over, the one named last changes fastest.
Arguments:
- records: float32 [8, 2, 1024, 2048], P('dp', None, None, 'freq'), may hold values from -6 to 6
- stem_weight: bfloat16 [256, 512], replicated, may hold values from -0.375 to 0.375
- conv_weight: bfloat16 [3, 3, 16, 512], replicated, may hold values from -0.875 to 0.875
- mix_weight: bfloat16 [3, 512, 512], replicated, may hold values from -0.25 to 0.25
- head_weight: float32 [512, 10], replicated, may hold values from -0.25 to 0.25
- labels: int32 [8], P('dp'), may hold values from 0 to 9
- band_bounds: int32 [33], replicated, may hold values from 0 to 1048576, as said below
Outputs:
- loss: float32 [], replicated
- grad_stem: float32 [256, 512], replicated
- grad_conv: float32 [3, 3, 16, 512], replicated
- grad_mix: float32 [3, 512, 512], replicated
- grad_head: float32 [512, 10], replicated
Inputs may be any that keep to these rules, and one draw needn't show every extreme that they name: `band_bounds`: strictly increasing multiples of 128; the first is 0 and the last is half of 2097152.
All inputs are finite; a program needn't handle non-finite values.
Results may differ from a plain program's by a relative error of at most 0.0018.
Values may be sent and summed in bfloat16 or wider, within the bound.
No kernel may reach another device: no remote copies, remote signals or barrier semaphores. Data moves between devices by JAX's collectives and lax.ppermute only.
A program may use at most 192 MiB of HBM per device.

v0:
```python
import jax
import jax.numpy as jnp
from jax import lax
from jax.sharding import PartitionSpec as P

POOL = 128
GROUP_WIDTH = 16
KW = 3


EXACT_DOTS = lax.Precision.HIGHEST
EPS = 1e-05


def with_halo(x, sides, width):
    for axis, dim in sides:
        devices, length = (lax.axis_size(axis), x.shape[dim])
        up = [(i, (i + 1) % devices) for i in range(devices - 1)]
        down = [(j, i) for i, j in up]
        last = lax.slice_in_dim(x, length - width, length, axis=dim)
        first = lax.slice_in_dim(x, 0, width, axis=dim)
        before = lax.ppermute(last, axis, up)
        after = lax.ppermute(first, axis, down)
        x = jnp.concatenate([before, x, after], axis=dim)
    return x


def first_section(signal):
    table_size = signal.shape[-2]
    row_index = lax.broadcasted_iota(jnp.int32, (table_size, table_size), 0)
    col_index = lax.broadcasted_iota(jnp.int32, (table_size, table_size), 1)
    angles = (col_index * (2 * row_index + 1) % (2 * table_size)).astype(jnp.float32) * (
        jnp.pi / table_size
    )
    cosine_table = jnp.cos(angles)
    sine_table = jnp.sin(angles)

    def table_product(table, values):
        return jnp.einsum("kn,...nm->...km", table, values, precision=EXACT_DOTS)

    return (table_product(cosine_table, signal), -table_product(sine_table, signal))


def apply_twiddle(real_part, imag_part, offset, total_len):
    row_count = real_part.shape[-2]
    col_count = real_part.shape[-1]
    row_index = lax.broadcasted_iota(jnp.int32, (row_count, col_count), 0)
    col_index = lax.broadcasted_iota(jnp.int32, (row_count, col_count), 1) + offset
    angles = (col_index * (2 * row_index + 1) % (2 * total_len)).astype(jnp.float32) * (
        jnp.pi / total_len
    )
    cosine_table = jnp.cos(angles)
    sine_table = jnp.sin(angles)
    return (
        real_part * cosine_table + imag_part * sine_table,
        imag_part * cosine_table - real_part * sine_table,
    )


def second_section(real_part, imag_part, columns):
    length = real_part.shape[-1]
    block_width = min(columns, 512)
    row_index = lax.broadcasted_iota(jnp.int32, (length, block_width), 0)

    def table_product(values, table):
        return jnp.einsum("...n,nc->...c", values, table, precision=EXACT_DOTS)

    def one_block(block_idx):
        col_index = (
            lax.broadcasted_iota(jnp.int32, (length, block_width), 1) + block_idx * block_width
        )
        angles = (row_index * col_index % length).astype(jnp.float32) * (2.0 * jnp.pi / length)
        cosine_table = jnp.cos(angles)
        sine_table = jnp.sin(angles)
        real_out = table_product(real_part, cosine_table) + table_product(imag_part, sine_table)
        imag_out = table_product(imag_part, cosine_table) - table_product(real_part, sine_table)
        return jnp.stack([real_out, imag_out])

    blocks = lax.map(one_block, jnp.arange(columns // block_width))
    blocks = jnp.moveaxis(blocks, 0, -2)
    return blocks.reshape(blocks.shape[:-2] + (columns,))


def bin_features(power, total_len):
    return jnp.swapaxes(jnp.log1p(power / total_len), 1, 2).astype(jnp.bfloat16)


def with_edges(values):
    return with_halo(values, (("freq", 1),), 1)


def group_mask(channels):
    row_group = lax.broadcasted_iota(jnp.int32, (channels, channels), 0) // GROUP_WIDTH
    col_group = lax.broadcasted_iota(jnp.int32, (channels, channels), 1) // GROUP_WIDTH
    return row_group == col_group


def dense_taps(tap_weights):
    channels = tap_weights.shape[-1]
    groups = channels // GROUP_WIDTH
    tiled = jnp.tile(tap_weights, (1, groups, 1))
    return jnp.where(group_mask(channels)[None], tiled, jnp.zeros_like(tiled))


def conv_forward(padded, dense_kernel, span_len):
    result = None
    for tap_idx in range(KW):
        window = padded[:, tap_idx : tap_idx + span_len]
        term = jnp.einsum(
            "rpc,cd->rpd", window, dense_kernel[tap_idx], preferred_element_type=jnp.float32
        )
        result = term if result is None else result + term
    return result


def conv_backward(grad_padded, dense_kernel, span_len):
    result = None
    for tap_idx in range(KW):
        shift_at = KW - 1 - tap_idx
        window = grad_padded[:, shift_at : shift_at + span_len]
        term = jnp.einsum(
            "rpd,cd->rpc", window, dense_kernel[tap_idx], preferred_element_type=jnp.float32
        )
        result = term if result is None else result + term
    return result


def conv_weight_grad(padded, grad_pre, span_len):
    channels = padded.shape[-1]
    groups = channels // GROUP_WIDTH
    picker = group_mask(channels).astype(jnp.float32).reshape(groups, GROUP_WIDTH, channels)[:, :1]
    tap_list = []
    for tap_idx in range(KW):
        window = padded[:, tap_idx : tap_idx + span_len]
        full_grad = jnp.einsum("rpc,rpd->cd", window, grad_pre, preferred_element_type=jnp.float32)
        tap_list.append(jnp.sum(full_grad.reshape(groups, GROUP_WIDTH, channels) * picker, axis=0))
    return jnp.stack(tap_list)


def local(records, stem_weight, conv_weight, mix_weight, head_weight, labels, band_bounds):
    freq_size = lax.axis_size("freq")
    my_place = lax.axis_index("freq")
    record_count = records.shape[0]
    first_len = records.shape[2]
    local_cols = records.shape[3]
    total_len = first_len * local_cols * freq_size
    col_offset = my_place * local_cols
    half_cols = local_cols * freq_size // 2
    real_part, imag_part = first_section(records)
    real_part, imag_part = apply_twiddle(real_part, imag_part, col_offset, total_len)
    stacked = jnp.stack([real_part, imag_part], axis=2)
    exchanged = lax.all_to_all(stacked, "freq", split_axis=3, concat_axis=4, tiled=True)
    spectrum = second_section(exchanged[:, :, 0], exchanged[:, :, 1], half_cols)
    power_both = spectrum[0] ** 2 + spectrum[1] ** 2
    power_a = power_both[:, 0]
    power_b = power_both[:, 1]
    feat_a = bin_features(power_a, total_len)
    feat_b = bin_features(power_b, total_len)
    exchanged = (
        lax.all_to_all(feat_a, "freq", split_axis=1, concat_axis=2, tiled=True),
        lax.all_to_all(feat_b, "freq", split_axis=1, concat_axis=2, tiled=True),
    )
    pieces = []
    for values in exchanged:
        pieces.append(values.reshape(values.shape[0], -1, POOL))
    positions = jnp.concatenate(pieces, axis=-1)
    stream = jnp.einsum("rpf,fc->rpc", positions, stem_weight, preferred_element_type=jnp.float32)
    local_len = stream.shape[1]
    channels = stream.shape[2]
    groups = channels // GROUP_WIDTH
    layer_count = conv_weight.shape[0]
    saved_layers = []
    for layer_idx in range(layer_count):
        dense_kernel = dense_taps(conv_weight[layer_idx])
        scales = lax.rsqrt(jnp.mean(stream * stream, axis=-1, keepdims=True) + EPS)
        normed = (stream * scales).astype(jnp.bfloat16)
        padded = with_edges(normed)
        preact = conv_forward(padded, dense_kernel, local_len)
        activated = jax.nn.silu(preact).astype(jnp.bfloat16)
        saved_layers.append((stream, padded, preact, activated, dense_kernel))
        stream = stream + jnp.einsum(
            "rpc,cd->rpd", activated, mix_weight[layer_idx], preferred_element_type=jnp.float32
        )
    starts = (my_place * local_len + lax.broadcasted_iota(jnp.int32, (local_len, 1), 0)) * POOL
    member = ((starts >= band_bounds[None, :-1]) & (starts < band_bounds[None, 1:])).astype(
        jnp.float32
    )
    counts = ((band_bounds[1:] - band_bounds[:-1]) // POOL).astype(jnp.float32)
    partial_value = jnp.einsum(
        "pg,rpgo->rgo",
        member,
        stream.reshape(record_count, local_len, groups, GROUP_WIDTH),
        precision=EXACT_DOTS,
    )
    band_sum = lax.psum(partial_value, "freq")
    pooled = (band_sum / counts[:, None]).reshape(record_count, channels)
    logits = jnp.dot(pooled, head_weight, precision=EXACT_DOTS)
    exponents = jnp.exp(logits)
    denominator = jnp.sum(exponents, axis=-1, keepdims=True)
    one_hot = (
        labels[:, None] == lax.broadcasted_iota(jnp.int32, (1, head_weight.shape[1]), 1)
    ).astype(jnp.float32)
    all_records = record_count * lax.axis_size("dp")
    lead_flag = (my_place == 0).astype(jnp.float32)
    loss_part = (
        jnp.sum(jnp.log(denominator[:, 0]) - jnp.sum(one_hot * logits, axis=-1))
        / all_records
        * lead_flag
    )
    grad_logits = (exponents / denominator - one_hot) / all_records
    head_part = jnp.dot(pooled.T, grad_logits, precision=EXACT_DOTS) * lead_flag
    grad_band = (
        jnp.dot(grad_logits, head_weight.T, precision=EXACT_DOTS).reshape(
            record_count, groups, GROUP_WIDTH
        )
        / counts[:, None]
    )
    grad_stream = (member[None, :, :, None] * grad_band[:, None]).reshape(
        record_count, local_len, channels
    )
    conv_grads = [None] * layer_count
    mix_grads = [None] * layer_count
    for layer_idx in reversed(range(layer_count)):
        stream_in, padded, preact, activated, dense_kernel = saved_layers[layer_idx]
        grad_out = grad_stream.astype(jnp.bfloat16)
        mix_grad = jnp.einsum(
            "rpc,rpd->cd", activated, grad_out, preferred_element_type=jnp.float32
        )
        grad_act = jnp.einsum(
            "rpd,cd->rpc", grad_out, mix_weight[layer_idx], preferred_element_type=jnp.float32
        )
        gate_value = jax.nn.sigmoid(preact)
        grad_pre = (grad_act * gate_value * (1.0 + preact * (1.0 - gate_value))).astype(
            jnp.bfloat16
        )
        grad_padded = with_edges(grad_pre)
        grad_normed = conv_backward(grad_padded, dense_kernel, local_len)
        tap_grads = conv_weight_grad(padded, grad_pre, local_len)
        conv_grads[layer_idx] = tap_grads
        mix_grads[layer_idx] = mix_grad
        scales = lax.rsqrt(jnp.mean(stream_in * stream_in, axis=-1, keepdims=True) + EPS)
        grad_stream = (
            grad_stream
            + scales * grad_normed
            - stream_in * scales**3 * jnp.mean(stream_in * grad_normed, axis=-1, keepdims=True)
        )
    grad_stem = jnp.einsum(
        "rpf,rpc->fc", positions.astype(jnp.float32), grad_stream, precision=EXACT_DOTS
    )
    loss_all, stem_all, conv_all, mix_all, head_all = lax.psum(
        (loss_part, grad_stem, jnp.stack(conv_grads), jnp.stack(mix_grads), head_part),
        ("dp", "freq"),
    )
    return (loss_all, stem_all, conv_all, mix_all, head_all)


def solution(mesh):
    in_specs = (P("dp", None, None, "freq"), P(), P(), P(), P(), P("dp"), P())
    out_specs = (P(), P(), P(), P(), P())
    return jax.shard_map(local, mesh=mesh, in_specs=in_specs, out_specs=out_specs, check_vma=False)
```

profile of v0, /device:TPU:0, one launch (start us, length us, event | category | flops | bytes accessed | tf_op | source)
XLA Modules:
  0.0 940.2 jit_solution(9593283226323650721)
XLA Ops:
  7.2 8.2 fusion.234
  15.5 29.5 %fusion.70 = f32[1024,2,512]{2,0,1:T(8,128)S(1)} fusion(f32[1,2,1024,512]{3,2,1,0:T(8,128)S(1)} %copy-done.53, s32[1024]{0:T(1024)S(1)} %multiply_add_fusion.1), kind=kOutput, calls=%fused_computation.65 | convolution fusion | flops 12899581952 | bytes 8392704 | tf_op jit(solution)/shard_map/kn,...nm->...km/dot_general | solution.py:39
  45.0 30.7 %fusion.67 = (f32[1,2,1,1024,512]{4,3,1,2,0:T(8,128)S(1)}, f32[1,2,1,1024,512]{4,3,1,2,0:T(8,128)S(1)}) fusion(f32[1024,2,512]{2,0,1:T(8,128)S(1)} %fusion.70, f32[1024,512]{1,0:T(8,128)S(1)} %get-tuple-element.152, f32[1024,512]{1,0:T(8,128)S(1)} %get-tuple-element.151, f32[1,2,1024,512]{3,2,1,0:T(8,128)S(1)} %copy-done.53, s32[1024]{0:T(1024)S(1)} %multiply_add_fusion.1), kind=kOutput, calls=%fused_computation.60 | convolution fusion | flops 12906921984 | bytes 20975616 | tf_op jit(solution)/shard_map/kn,...nm->...km/dot_general | solution.py:39
  76.7 13.4 %copy.85 = f32[1,2,2,1024,512]{4,1,2,0,3:T(2,128)} copy(f32[1,2,2,1024,512]{4,3,1,2,0:T(8,128)S(1)} %pad_maximum_fusion) | data formatting | bytes 16777216 | tf_op jit(solution)/shard_map/stack | solution.py:151
  90.0 6.4 all-to-all-start
  98.5 182.1 %all-to-all-done = f32[1,2,2,1024,512]{4,1,2,0,3:T(2,128)} async-done(((f32[1,2,2,1024,512]{4,1,2,0,3:T(2,128)}), f32[1,2,2,1024,512]{4,1,2,0,3:T(2,128)}, u32[]{:S(2)}, u32[]{:S(2)}) %all-to-all-start) | async-done | bytes 8388640 | tf_op jit(solution)/shard_map/all_to_all | solution.py:152
  280.6 12.0 %copy.86 = f32[1,2,2,256,4,512]{5,4,3,1,2,0:T(4,128)} copy(f32[1,2,2,256,4,512]{5,1,2,3,4,0:T(2,128)} %bitcast.17) | data formatting | bytes 16777216 | tf_op jit(solution)/shard_map/all_to_all | solution.py:152
  292.7 11.0 %all_to_all.38 = f32[1,2,2,256,2048]{4,3,1,2,0:T(8,128)} reshape(f32[1,2,2,256,4,512]{5,4,3,1,2,0:T(4,128)} %copy.86) | data formatting | bytes 16777216 | tf_op jit(solution)/shard_map/all_to_all | solution.py:152
  303.6 7.8 slice_bitcast_fusion
  311.4 199.1 %while.13 = (s32[]{:T(128)}, f32[2,2,1,2,256,512]{4,5,0,3,2,1:T(8,128)}, s32[2]{0:T(128)S(1)}, f32[1,2,256,2048]{3,2,1,0:T(8,128)}, f32[1,2,256,2048]{3,2,1,0:T(8,128)}, /*index=5*/s32[]{:T(128)}, s32[1]{0:T(128)}) while((s32[]{:T(128)}, f32[2,2,1,2,256,512]{4,5,0,3,2,1:T(8,128)}, s32[2]{0:T(128)S(1)}, ...), condition=%wide.region_1.2_spmd.clone, body=%wide.region_0.1_spmd.clone.sunk | while | flops 25829572608 | bytes 60828320 | solution.py:79
  312.9 24.7 %fusion.349 = f32[512,2,256]{2,0,1:T(8,128)S(1)} fusion(f32[1,2,256,2048]{3,2,1,0:T(8,128)} %get-tuple-element.220, s32[512]{0:T(512)S(1)} %iota_add_fusion.3), kind=kOutput, calls=%fused_computation.9.clone.1 | convolution fusion | flops 6457131008 | bytes 5244928 | tf_op jit(solution)/shard_map/while/body/eval_jaxpr/...n,nc->...c/dot_general | solution.py:66
  337.5 22.6 %fusion.350 = f32[1,1,2,256,512]{3,4,2,1,0:T(8,128)S(1)} fusion(f32[512,2,256]{2,0,1:T(8,128)S(1)} %fusion.349, f32[1,2,256,2048]{3,2,1,0:T(8,128)S(1)} %copy-done.36, s32[512]{0:T(512)S(1)} %iota_add_fusion.3), kind=kOutput, calls=%fused_computation.28.clone.1 | convolution fusion | flops 6457393152 | bytes 6293504 | tf_op jit(solution)/shard_map/while/body/eval_jaxpr/...n,nc->...c/dot_general | solution.py:66
  360.1 22.7 %fusion.347 = f32[512,2,256]{2,0,1:T(8,128)S(1)} fusion(f32[1,2,256,2048]{3,2,1,0:T(8,128)S(1)} %copy-done.35, s32[512]{0:T(512)S(1)} %iota_add_fusion.3), kind=kOutput, calls=%fused_computation.7.clone.1 | convolution fusion | flops 6457131008 | bytes 5244928 | tf_op jit(solution)/shard_map/while/body/eval_jaxpr/...n,nc->...c/dot_general | solution.py:66
  382.8 22.3 %fusion.348 = f32[1,1,2,256,512]{3,4,2,1,0:T(8,128)S(1)} fusion(f32[512,2,256]{2,0,1:T(8,128)S(1)} %fusion.347, f32[1,2,256,2048]{3,2,1,0:T(8,128)S(1)} %copy-done.36, s32[512]{0:T(512)S(1)} %iota_add_fusion.3), kind=kOutput, calls=%fused_computation.30.clone.1 | convolution fusion | flops 6457393152 | bytes 6293504 | tf_op jit(solution)/shard_map/while/body/eval_jaxpr/...n,nc->...c/dot_general | solution.py:66
  408.2 24.6 %fusion.349 = f32[512,2,256]{2,0,1:T(8,128)S(1)} fusion(f32[1,2,256,2048]{3,2,1,0:T(8,128)} %get-tuple-element.220, s32[512]{0:T(512)S(1)} %iota_add_fusion.3), kind=kOutput, calls=%fused_computation.9.clone.1 | convolution fusion | flops 6457131008 | bytes 5244928 | tf_op jit(solution)/shard_map/while/body/eval_jaxpr/...n,nc->...c/dot_general | solution.py:66
  432.8 22.6 %fusion.350 = f32[1,1,2,256,512]{3,4,2,1,0:T(8,128)S(1)} fusion(f32[512,2,256]{2,0,1:T(8,128)S(1)} %fusion.349, f32[1,2,256,2048]{3,2,1,0:T(8,128)S(1)} %copy-done.36, s32[512]{0:T(512)S(1)} %iota_add_fusion.3), kind=kOutput, calls=%fused_computation.28.clone.1 | convolution fusion | flops 6457393152 | bytes 6293504 | tf_op jit(solution)/shard_map/while/body/eval_jaxpr/...n,nc->...c/dot_general | solution.py:66
  455.5 22.6 %fusion.347 = f32[512,2,256]{2,0,1:T(8,128)S(1)} fusion(f32[1,2,256,2048]{3,2,1,0:T(8,128)S(1)} %copy-done.35, s32[512]{0:T(512)S(1)} %iota_add_fusion.3), kind=kOutput, calls=%fused_computation.7.clone.1 | convolution fusion | flops 6457131008 | bytes 5244928 | tf_op jit(solution)/shard_map/while/body/eval_jaxpr/...n,nc->...c/dot_general | solution.py:66
  478.1 22.3 %fusion.348 = f32[1,1,2,256,512]{3,4,2,1,0:T(8,128)S(1)} fusion(f32[512,2,256]{2,0,1:T(8,128)S(1)} %fusion.347, f32[1,2,256,2048]{3,2,1,0:T(8,128)S(1)} %copy-done.36, s32[512]{0:T(512)S(1)} %iota_add_fusion.3), kind=kOutput, calls=%fused_computation.30.clone.1 | convolution fusion | flops 6457393152 | bytes 6293504 | tf_op jit(solution)/shard_map/while/body/eval_jaxpr/...n,nc->...c/dot_general | solution.py:66
  526.1 5.4 copy.94
  537.6 4.6 all-to-all-start.2
  546.5 9.4 all-to-all-done.2
  623.7 4.6 collective-permute-start.4
  656.0 5.4 copy.93
  661.4 4.8 fusion.235
  666.2 20.1 %psum.42 = f32[1,32,16]{2,1,0:T(8,128)S(1)} all-reduce(f32[1,32,16]{2,1,0:T(8,128)S(1)} %bitcast.473), channel_id=1, replica_groups=mesh['dp'=8,'freq'=4] {'freq'}, use_global_device_ids=true, to_apply=%region_5.6 | all-reduce | flops 512 | bytes 4096 | tf_op jit(solution)/shard_map/psum | solution.py:195
  689.9 5.6 multiply_convert_fusion.2
  695.5 4.7 fusion.250
  701.6 4.8 collective-permute-start.7
  742.4 4.5 collective-permute-start.9
  769.1 4.8 collective-permute-start.11
  786.4 39.7 %all-reduce = (f32[]{:T(128)}, f32[512,10]{0,1:T(8,128)}) all-reduce(f32[]{:T(128)S(6)} %mul.488, f32[512,10]{0,1:T(8,128)S(1)} %multiply_multiply_fusion), channel_id=1, replica_groups=mesh['dp'=8,'freq'=4] {'dp','freq'}, use_global_device_ids=true, to_apply=%region_8.9 | all-reduce | flops 5121 | bytes 40968 | tf_op jit(solution)/shard_map/psum | solution.py:250
  826.1 99.6 %all-reduce.4.cloned.1.call-done = (f32[256,512]{1,0:T(8,128)}, f32[3,3,16,512]{3,2,1,0:T(8,128)}, f32[3,512,512]{2,1,0:T(8,128)}) async-done(((f32[256,512]{1,0:T(8,128)}, f32[3,3,16,512]{3,2,1,0:T(8,128)}, f32[3,512,512]{2,1,0:T(8,128)}), (f32[256,512]{1,0:T(8,128)}, f32[3,3,16,512]{3,2,1,0:T(8,128)}, f32[3,512,512]{2,1,0:T(8,128)})) %all-reduce.4.cloned.1.call-update) | async-done | bytes 3964944 | tf_op jit(solution)/shard_map/psum | solution.py:250
  (269 shorter events, 208.8 us)
Async XLA Ops:
  7.2 550.0 %copy-start = (bf16[256,512]{1,0:T(8,128)(2,1)S(1)}, bf16[256,512]{1,0:T(8,128)(2,1)}, u32[]{:S(2)}) copy-start(bf16[256,512]{1,0:T(8,128)(2,1)} %param.10) | copy-start | bytes 786436
  7.2 8.2 copy-start.53
  90.0 190.6 %all-to-all-start = ((f32[1,2,2,1024,512]{4,1,2,0,3:T(2,128)}), f32[1,2,2,1024,512]{4,1,2,0,3:T(2,128)}, u32[]{:S(2)}, u32[]{:S(2)}) async-start(f32[1,2,2,1024,512]{4,1,2,0,3:T(2,128)} %copy.85), calls=%async_computation | async-start | bytes 16777216 | tf_op jit(solution)/shard_map/all_to_all | solution.py:152
  312.9 24.7 %copy-start.36 = (f32[1,2,256,2048]{3,2,1,0:T(8,128)S(1)}, f32[1,2,256,2048]{3,2,1,0:T(8,128)}, u32[]{:S(2)}) copy-start(f32[1,2,256,2048]{3,2,1,0:T(8,128)} %get-tuple-element.219) | copy-start | bytes 12582916 | tf_op jit(solution)/shard_map/while
  337.5 22.6 %copy-start.35 = (f32[1,2,256,2048]{3,2,1,0:T(8,128)S(1)}, f32[1,2,256,2048]{3,2,1,0:T(8,128)}, u32[]{:S(2)}) copy-start(f32[1,2,256,2048]{3,2,1,0:T(8,128)} %get-tuple-element.220) | copy-start | bytes 12582916 | tf_op jit(solution)/shard_map/while
  408.2 24.6 %copy-start.36 = (f32[1,2,256,2048]{3,2,1,0:T(8,128)S(1)}, f32[1,2,256,2048]{3,2,1,0:T(8,128)}, u32[]{:S(2)}) copy-start(f32[1,2,256,2048]{3,2,1,0:T(8,128)} %get-tuple-element.219) | copy-start | bytes 12582916 | tf_op jit(solution)/shard_map/while
  432.8 22.6 %copy-start.35 = (f32[1,2,256,2048]{3,2,1,0:T(8,128)S(1)}, f32[1,2,256,2048]{3,2,1,0:T(8,128)}, u32[]{:S(2)}) copy-start(f32[1,2,256,2048]{3,2,1,0:T(8,128)} %get-tuple-element.220) | copy-start | bytes 12582916 | tf_op jit(solution)/shard_map/while
  520.0 17.7 %all-to-all-start.1 = ((bf16[4,2,32768]{2,1,0:T(2,128)(2,1)}), bf16[4,2,32768]{2,1,0:T(2,128)(2,1)S(1)}, u32[]{:S(2)}, u32[]{:S(2)}) async-start(bf16[4,2,32768]{2,1,0:T(2,128)(2,1)} %reshape.864), calls=%async_computation.1 | async-start | bytes 1048576 | tf_op jit(solution)/shard_map/all_to_all | solution.py:160
  531.5 10.7 %copy-start.47 = (bf16[3,3,16,512]{3,2,1,0:T(8,128)(2,1)S(1)}, bf16[3,3,16,512]{3,2,1,0:T(8,128)(2,1)}, u32[]{:S(2)}) copy-start(bf16[3,3,16,512]{3,2,1,0:T(8,128)(2,1)} %param.11) | copy-start | bytes 442372
  537.6 18.3 %all-to-all-start.2 = ((bf16[4,2,32768]{2,1,0:T(2,128)(2,1)}), bf16[4,2,32768]{2,1,0:T(2,128)(2,1)S(1)}, u32[]{:S(2)}, u32[]{:S(2)}) async-start(bf16[4,2,32768]{2,1,0:T(2,128)(2,1)} %reshape.862), calls=%async_computation.2 | async-start | bytes 1048576 | tf_op jit(solution)/shard_map/all_to_all | solution.py:161
  542.2 383.5 %all-reduce.4.cloned.1.call-start = ((), (), s32[]{:S(2)}) async-start(), calls=%async_computation.3 | async-start | bytes 7929856 | tf_op jit(solution)/shard_map/psum | solution.py:250
  546.5 11.4 %copy-start.25 = (bf16[1,2048,128]{2,1,0:T(8,128)(2,1)}, bf16[1,2048,128]{2,1,0:T(8,128)(2,1)S(1)}, u32[]{:S(2)}) copy-start(bf16[1,2048,128]{2,1,0:T(8,128)(2,1)S(1)} %reshape.828) | copy-start | bytes 1572868
  559.0 15.6 %copy-start.17 = (bf16[1,2048,512]{2,1,0:T(8,128)(2,1)}, bf16[1,2048,512]{2,1,0:T(8,128)(2,1)S(1)}, u32[]{:S(2)}) copy-start(bf16[1,2048,512]{2,1,0:T(8,128)(2,1)S(1)} %fusion.325) | copy-start | bytes 6291460
  561.1 10.9 %collective-permute-start = (bf16[1,1,512]{2,1,0:T(2,128)(2,1)S(1)}, bf16[1,1,512]{2,1,0:T(2,128)(2,1)S(1)}, u32[]{:S(2)}, u32[]{:S(2)}) collective-permute-start(bf16[1,1,512]{2,1,0:T(2,128)(2,1)S(1)} %get-tuple-element.134), channel_id=1, source_target_pairs={{0,1},{1,2},{2,3},{4,5},{5,6},{6,7},{8,9},{9,10},{10,11},{12,13},{... | collective-permute-start | bytes 3080 | tf_op jit(solution)/shard_map/ppermute | solution.py:22
  566.8 7.7 collective-permute-start.1
  580.6 30.1 %copy-start.15 = (bf16[1,2048,512]{2,1,0:T(8,128)(2,1)}, bf16[1,2048,512]{2,1,0:T(8,128)(2,1)S(1)}, u32[]{:S(2)}) copy-start(bf16[1,2048,512]{2,1,0:T(8,128)(2,1)S(1)} %fusion.324) | copy-start | bytes 6291460
  582.8 10.3 %copy-start.18 = (bf16[1,2048,512]{2,1,0:T(8,128)(2,1)S(1)}, bf16[1,2048,512]{2,1,0:T(8,128)(2,1)}, u32[]{:S(2)}) copy-start(bf16[1,2048,512]{2,1,0:T(8,128)(2,1)} %copy-done.17) | copy-start | bytes 6291460
  587.3 21.0 %collective-permute-start.2 = (bf16[1,1,512]{2,1,0:T(2,128)(2,1)S(1)}, bf16[1,1,512]{2,1,0:T(2,128)(2,1)S(1)}, u32[]{:S(2)}, u32[]{:S(2)}) collective-permute-start(bf16[1,1,512]{2,1,0:T(2,128)(2,1)S(1)} %get-tuple-element.132), channel_id=1, source_target_pairs={{0,1},{1,2},{2,3},{4,5},{5,6},{6,7},{8,9},{9,10},{10,11},{12,13},{... | collective-permute-start | bytes 3080 | tf_op jit(solution)/shard_map/ppermute | solution.py:22
  591.8 18.9 %collective-permute-start.3 = (bf16[1,1,512]{2,1,0:T(2,128)(2,1)S(1)}, bf16[1,1,512]{2,1,0:T(2,128)(2,1)S(1)}, u32[]{:S(2)}, u32[]{:S(2)}) collective-permute-start(bf16[1,1,512]{2,1,0:T(2,128)(2,1)S(1)} %get-tuple-element.131), channel_id=1, source_target_pairs={{1,0},{2,1},{3,2},{5,4},{6,5},{7,6},{9,8},{10,9},{11,10},{13,12},{... | collective-permute-start | bytes 3080 | tf_op jit(solution)/shard_map/ppermute | solution.py:23
  619.1 10.4 %copy-start.16 = (bf16[1,2048,512]{2,1,0:T(8,128)(2,1)S(1)}, bf16[1,2048,512]{2,1,0:T(8,128)(2,1)}, u32[]{:S(2)}) copy-start(bf16[1,2048,512]{2,1,0:T(8,128)(2,1)} %copy-done.15) | copy-start | bytes 6291460
  623.7 20.8 %collective-permute-start.4 = (bf16[1,1,512]{2,1,0:T(2,128)(2,1)S(1)}, bf16[1,1,512]{2,1,0:T(2,128)(2,1)S(1)}, u32[]{:S(2)}, u32[]{:S(2)}) collective-permute-start(bf16[1,1,512]{2,1,0:T(2,128)(2,1)S(1)} %get-tuple-element.130), channel_id=1, source_target_pairs={{0,1},{1,2},{2,3},{4,5},{5,6},{6,7},{8,9},{9,10},{10,11},{12,13},{... | collective-permute-start | bytes 3080 | tf_op jit(solution)/shard_map/ppermute | solution.py:22
  628.2 18.7 %collective-permute-start.5 = (bf16[1,1,512]{2,1,0:T(2,128)(2,1)S(1)}, bf16[1,1,512]{2,1,0:T(2,128)(2,1)S(1)}, u32[]{:S(2)}, u32[]{:S(2)}) collective-permute-start(bf16[1,1,512]{2,1,0:T(2,128)(2,1)S(1)} %get-tuple-element.129), channel_id=1, source_target_pairs={{1,0},{2,1},{3,2},{5,4},{6,5},{7,6},{9,8},{10,9},{11,10},{13,12},{... | collective-permute-start | bytes 3080 | tf_op jit(solution)/shard_map/ppermute | solution.py:23
  661.4 24.9 %copy-start.51 = (f32[32]{0:T(128)S(1)}, f32[32]{0:T(128)}, u32[]{:S(2)}) copy-start(f32[32]{0:T(128)} %get-tuple-element.153) | copy-start | bytes 388
  661.4 25.0 %copy-start.49 = (f32[512,10]{0,1:T(8,128)S(1)}, f32[512,10]{0,1:T(8,128)}, u32[]{:S(2)}) copy-start(f32[512,10]{0,1:T(8,128)} %param.13) | copy-start | bytes 61444
  661.4 26.6 %copy-start.44 = (f32[32,16,10]{1,0,2:T(8,128)S(1)}, f32[32,16,10]{1,0,2:T(8,128)}, u32[]{:S(2)}) copy-start(f32[32,16,10]{1,0,2:T(8,128)} %dot_general.203) | copy-start | bytes 61444
  700.3 27.4 %collective-permute-start.6 = (bf16[1,1,512]{2,1,0:T(2,128)(2,1)S(1)}, bf16[1,1,512]{2,1,0:T(2,128)(2,1)S(1)}, u32[]{:S(2)}, u32[]{:S(2)}) collective-permute-start(bf16[1,1,512]{2,1,0:T(2,128)(2,1)S(1)} %get-tuple-element.128), channel_id=1, source_target_pairs={{1,0},{2,1},{3,2},{5,4},{6,5},{7,6},{9,8},{10,9},{11,10},{13,12},{... | collective-permute-start | bytes 3080 | tf_op jit(solution)/shard_map/ppermute | solution.py:23
  701.6 27.4 %collective-permute-start.7 = (bf16[1,1,512]{2,1,0:T(2,128)(2,1)S(1)}, bf16[1,1,512]{2,1,0:T(2,128)(2,1)S(1)}, u32[]{:S(2)}, u32[]{:S(2)}) collective-permute-start(bf16[1,1,512]{2,1,0:T(2,128)(2,1)S(1)} %get-tuple-element.127), channel_id=1, source_target_pairs={{0,1},{1,2},{2,3},{4,5},{5,6},{6,7},{8,9},{9,10},{10,11},{12,13},{... | collective-permute-start | bytes 3080 | tf_op jit(solution)/shard_map/ppermute | solution.py:22
  741.1 10.3 %collective-permute-start.8 = (bf16[1,1,512]{2,1,0:T(2,128)(2,1)S(1)}, bf16[1,1,512]{2,1,0:T(2,128)(2,1)S(1)}, u32[]{:S(2)}, u32[]{:S(2)}) collective-permute-start(bf16[1,1,512]{2,1,0:T(2,128)(2,1)S(1)} %get-tuple-element.126), channel_id=1, source_target_pairs={{1,0},{2,1},{3,2},{5,4},{6,5},{7,6},{9,8},{10,9},{11,10},{13,12},{... | collective-permute-start | bytes 3080 | tf_op jit(solution)/shard_map/ppermute | solution.py:23
  742.4 10.3 %collective-permute-start.9 = (bf16[1,1,512]{2,1,0:T(2,128)(2,1)S(1)}, bf16[1,1,512]{2,1,0:T(2,128)(2,1)S(1)}, u32[]{:S(2)}, u32[]{:S(2)}) collective-permute-start(bf16[1,1,512]{2,1,0:T(2,128)(2,1)S(1)} %get-tuple-element.125), channel_id=1, source_target_pairs={{0,1},{1,2},{2,3},{4,5},{5,6},{6,7},{8,9},{9,10},{10,11},{12,13},{... | collective-permute-start | bytes 3080 | tf_op jit(solution)/shard_map/ppermute | solution.py:22
  767.8 8.8 collective-permute-start.10
  769.1 8.8 collective-permute-start.11
  784.9 148.2 %copy-start.1 = (bf16[256,512]{1,0:T(8,128)(2,1)S(1)}, bf16[256,512]{1,0:T(8,128)(2,1)}, u32[]{:S(2)}) copy-start(bf16[256,512]{1,0:T(8,128)(2,1)} %param.10) | copy-start | bytes 786436
  (41 other events, 123.7 us)
Sparse Core Ops, SparseCore 0:
  785.0 140.6 all-reduce.3
where the time goes:
time: 949 us; the launch traced here: 940 us
  matrix products  341 us (36%)
  waiting for transfers between devices  292 us (31%)
  local copies, waits for them, and re-layouts  120 us (13%)
  blocking collectives  59.8 us (6%)
  other arithmetic  52.3 us (6%)
  starting transfers between devices  46.7 us (5%)
  between operations  17.4 us (2%)
  loops' own time  10.6 us (1%)
    dot_general x8, matrix products, table_product(): return jnp.einsum('...n,nc->...c', values, table, precision=EXACT_DOTS)  184 us
    all_to_all x1, waiting for transfers between devices, local(): lax.all_to_all(stacked, 'freq', split_axis=3, concat_axis=4, tiled=True)  182 us
    psum x1, waiting for transfers between devices, local(): lax.psum((loss_part, grad_stem, jnp.stack(conv_grads), jnp.stack(mix_grad...  99.6 us
    dot_general x2, matrix products, table_product(): return jnp.einsum('kn,...nm->...km', table, values, precision=EXACT_DOTS)  60.2 us
    psum x1, blocking collectives, local(): lax.psum((loss_part, grad_stem, jnp.stack(conv_grads), jnp.stack(mix_grad...  39.7 us
    dot_general x9, matrix products, conv_forward(): jnp.einsum('rpc,cd->rpd', window, dense_kernel[tap_idx], preferred_elemen...  28.5 us
    ppermute x6, starting transfers between devices, with_halo(): before = lax.ppermute(last, axis, up)  24.4 us
    dot_general x6, local copies, waits for them, and re-layouts, conv_weight_grad(): jnp.einsum('rpc,rpd->cd', window, grad_pre, preferred_element_type=jnp.fl...  24.3 us
  transfers between devices with their start and end apart: 16, of which 4 were waited for; matrix products, arithmetic and copies ran while one was open for 10% of the time, Pallas kernels for 0%

commit v1 on v0

v1 whole, which is shorter than its diff:
```python
import functools

import jax
import jax.numpy as jnp
import numpy as np
from jax import lax
from jax.experimental import pallas as pl
from jax.experimental.pallas import tpu as pltpu
from jax.sharding import PartitionSpec as P

POOL = 128
GROUP_WIDTH = 16
KW = 3
EPS = 1e-05
LANES = 128
HALF_MXU = 256
HALO = 16
TILE = 256
F32 = jnp.float32
BF16 = jnp.bfloat16


def split16(values):
    high = values.astype(BF16)
    return high, (values - high.astype(F32)).astype(BF16)


def table_pair(values):
    high = values.astype(jnp.bfloat16)
    return np.stack([high, (values - high.astype(np.float64)).astype(jnp.bfloat16)])


def first_tables(first_len, second_len):
    total_len = first_len * second_len
    rows = np.arange(first_len // 2)
    odd = 2 * rows + 1
    angles = (np.outer(np.arange(first_len), odd) % (2 * first_len)) * (np.pi / first_len)
    twiddles = (np.outer(np.arange(second_len), odd) % (2 * total_len)) * (np.pi / total_len)

    def by_block(a, b):
        blocks = first_len // 2 // LANES
        a = a.reshape(a.shape[0], blocks, 1, LANES)
        b = b.reshape(b.shape[0], blocks, 1, LANES)
        return np.concatenate([a, b], axis=2).reshape(a.shape[0], -1)

    section = table_pair(by_block(np.cos(angles), -np.sin(angles)))
    twiddle = by_block(np.cos(twiddles), np.sin(twiddles)).astype(np.float32)
    return section, twiddle


def second_tables(second_len):
    quarter = second_len // 4
    idx = np.arange(quarter)
    angles = np.outer(np.arange(1, 4), idx) * (2 * np.pi / second_len)
    spread = np.stack([np.cos(angles), np.sin(angles)], axis=1)[..., None] * np.ones(LANES)
    order = np.concatenate([idx[: quarter // 2], idx[quarter // 2 :][::-1]])
    inner = (np.outer(order, idx) % quarter) * (2 * np.pi / quarter)
    table = table_pair(np.concatenate([np.cos(inner), np.sin(inner)], axis=1))
    flip = np.eye(LANES)[::-1].astype(jnp.bfloat16)
    return spread.astype(np.float32), table, flip


def level_of(exponent, mantissa):
    return mantissa * jnp.exp(exponent * np.log(2.0).astype(np.float32)) * (1.0 / (16384.0 * 32767.0))


def first_kernel(devices, place_ref, x_ref, table_ref, twiddle_ref, *refs):
    outs, codes = refs[:devices], refs[devices]
    signals, _, tile = x_ref.shape
    row = lax.broadcasted_iota(jnp.int32, (HALO, 2 * LANES), 0)
    for signal in range(signals):
        high, low = split16(x_ref[signal].T)
        both = jnp.dot(high, table_ref[0], preferred_element_type=F32)
        both += jnp.dot(low, table_ref[0], preferred_element_type=F32)
        both += jnp.dot(high, table_ref[1], preferred_element_type=F32)
        for at in range(0, both.shape[1], 2 * LANES):
            real, imag = both[:, at : at + LANES], both[:, at + LANES : at + 2 * LANES]
            cosine = twiddle_ref[:, at : at + LANES]
            sine = twiddle_ref[:, at + LANES : at + 2 * LANES]
            turned = jnp.concatenate(
                [real * cosine + imag * sine, imag * cosine - real * sine], axis=1
            )
            top = jnp.maximum(jnp.max(jnp.abs(turned), axis=0, keepdims=True), 1e-20)
            exponent = jnp.ceil(jnp.log(top) * (1.0 / np.log(2.0)))
            mantissa = jnp.floor(
                top * jnp.exp(-exponent * np.log(2.0).astype(np.float32)) * 16384.0
            ) + 1.0
            level = 1.0 / level_of(exponent, mantissa)
            coded = jnp.round(turned * level).astype(jnp.int32)
            head = jnp.where(row == 0, exponent, jnp.where(row == 1, mantissa, 0.0))
            codes[signal, :tile, at : at + 2 * LANES] = coded.astype(jnp.int16)
            codes[signal, tile:, at : at + 2 * LANES] = head.astype(jnp.int32).astype(jnp.int16)
    for shift in range(devices):
        to = (place_ref[0] + shift) % devices
        lanes = pl.ds(pl.multiple_of((to // signals) * 2 * LANES, 2 * LANES), 2 * LANES)
        outs[shift][...] = codes[to % signals, :, lanes]


def first_section(place, records, at, signals, devices, section, twiddle):
    first_len, cols = records.shape[-2:]
    tile = 256
    steps = cols // tile
    width = section.shape[-1]
    shape = jax.ShapeDtypeStruct((steps * (tile + HALO), 2 * LANES), jnp.int16)
    return pl.pallas_call(
        functools.partial(first_kernel, devices),
        out_shape=[shape] * devices,
        grid_spec=pltpu.PrefetchScalarGridSpec(
            num_scalar_prefetch=1,
            grid=(steps,),
            in_specs=[
                pl.BlockSpec((signals, first_len, tile), lambda i, s: (at, 0, i)),
                pl.BlockSpec(section.shape, lambda i, s: (0, 0, 0)),
                pl.BlockSpec((tile, width), lambda i, s: (s[0] * steps + i, 0)),
            ],
            out_specs=[pl.BlockSpec((tile + HALO, 2 * LANES), lambda i, s: (i, 0))] * devices,
            scratch_shapes=[pltpu.VMEM((signals, tile + HALO, width), jnp.int16)],
        ),
        compiler_params=pltpu.CompilerParams(vmem_limit_bytes=60 * 1024 * 1024),
        cost_estimate=pl.CostEstimate(
            flops=6 * signals * first_len * cols * width, bytes_accessed=2**23, transcendentals=0
        ),
        name="first_section",
    )(place, records, section, twiddle)


def second_kernel(devices, total_len, place_ref, *refs):
    received, refs = refs[:devices], refs[devices:]
    (spread_ref, table_ref, flip_ref), refs = refs[:3], refs[3:]
    outs, (signal, right, rest, packed) = refs[:devices], refs[devices:]
    place = place_ref[0]
    cols = signal.shape[0] // devices
    tile = 256
    quarter = signal.shape[0] // 4
    run = quarter // 2 // devices
    for shift in range(devices):
        source = (place - shift + devices) % devices
        for i in range(cols // tile):
            at = i * (tile + HALO)
            head = received[shift][at + tile : at + tile + HALO, :].astype(jnp.int32).astype(F32)
            values = received[shift][at : at + tile, :].astype(jnp.int32).astype(F32)
            rows = pl.ds(pl.multiple_of(source * cols + i * tile, tile), tile)
            signal[rows, :] = values * level_of(head[0:1], head[1:2])
    step = min(quarter, 128)
    for at in range(0, quarter, step):
        parts = [signal[g * quarter + at : g * quarter + at + step, :] for g in range(4)]
        re = [v[:, :LANES] for v in parts]
        im = [v[:, LANES:] for v in parts]
        sum_r, dif_r = re[0] + re[2], re[0] - re[2]
        sum_i, dif_i = im[0] + im[2], im[0] - im[2]
        odd_r, odm_r = re[1] + re[3], re[1] - re[3]
        odd_i, odm_i = im[1] + im[3], im[1] - im[3]
        turned = [
            (sum_r + odd_r, sum_i + odd_i),
            (dif_r + odm_i, dif_i - odm_r),
            (sum_r - odd_r, sum_i - odd_i),
            (dif_r - odm_i, dif_i + odm_r),
        ]
        for c in range(4):
            real, imag = turned[c]
            if c:
                cosine = spread_ref[c - 1, 0, at : at + step, :]
                sine = spread_ref[c - 1, 1, at : at + step, :]
                real, imag = real * cosine + imag * sine, imag * cosine - real * sine
            first = slice(2 * LANES * c, 2 * LANES * c + LANES)
            second = slice(2 * LANES * c + LANES, 2 * LANES * (c + 1))
            for ref, r, i in zip((right, rest), split16(real), split16(imag)):
                ref[at : at + step, first] = r
                ref[at : at + step, second] = i
                ref[quarter + at : quarter + at + step, first] = i
                ref[quarter + at : quarter + at + step, second] = -r
    row = lax.broadcasted_iota(jnp.int32, (HALO, LANES), 0)
    edges = [jnp.zeros((HALO, LANES), F32) for _ in range(devices)]
    for c in range(4):
        lanes = slice(2 * LANES * c, 2 * LANES * (c + 1))
        both = jnp.dot(table_ref[0], right[:, lanes], preferred_element_type=F32)
        both += jnp.dot(table_ref[0], rest[:, lanes], preferred_element_type=F32)
        both += jnp.dot(table_ref[1], right[:, lanes], preferred_element_type=F32)
        power = both[:, :LANES] ** 2 + both[:, LANES:] ** 2
        features = jnp.log1p(power * (1.0 / total_len))
        low = features[: quarter // 2].astype(BF16)
        high = jnp.dot(
            features[quarter // 2 :].astype(BF16), flip_ref[...], preferred_element_type=F32
        )
        for part, values, group in ((0, low, c), (1, high.astype(BF16), 4 + 3 - c)):
            wide = values.astype(F32)
            for to in range(devices):
                packed[to, group * run : (group + 1) * run, :] = values[to * run : (to + 1) * run]
                if group % 4 == 3 and to > 0:
                    edges[to] = jnp.where(
                        row == 2 * part, wide[to * run - 1 : to * run], edges[to]
                    )
                if group % 4 == 0 and to < devices - 1:
                    edges[to] = jnp.where(
                        row == 2 * part + 1, wide[(to + 1) * run : (to + 1) * run + 1], edges[to]
                    )
    for to in range(devices):
        packed[to, 8 * run :, :] = edges[to].astype(BF16)
    for shift in range(devices):
        outs[shift][...] = packed[(place + shift) % devices]


def second_section(place, received, second_len, total_len, spread, table, flip):
    devices = len(received)
    quarter = second_len // 4
    run = quarter // 2 // devices
    shape = (8 * run + HALO, LANES)
    vmem = pl.BlockSpec(memory_space=pltpu.VMEM)
    return pl.pallas_call(
        functools.partial(second_kernel, devices, total_len),
        out_shape=[jax.ShapeDtypeStruct(shape, BF16)] * devices,
        in_specs=[pl.BlockSpec(memory_space=pltpu.SMEM)] + [vmem] * (devices + 3),
        out_specs=[vmem] * devices,
        scratch_shapes=[
            pltpu.VMEM((second_len, 2 * LANES), F32),
            pltpu.VMEM((2 * quarter, 8 * LANES), BF16),
            pltpu.VMEM((2 * quarter, 8 * LANES), BF16),
            pltpu.VMEM((devices,) + shape, BF16),
        ],
        compiler_params=pltpu.CompilerParams(vmem_limit_bytes=32 * 1024 * 1024),
        cost_estimate=pl.CostEstimate(
            flops=96 * LANES * quarter * quarter, bytes_accessed=2**23, transcendentals=0
        ),
        name="second_section",
    )(place, *received, spread, table, flip)


def position_column(start, run, at, rows):
    row = at + lax.broadcasted_iota(jnp.int32, (rows, 1), 0)
    return start + row // run + 32 * (row % run)


def halo_column(start, count):
    row = lax.broadcasted_iota(jnp.int32, (HALO, 1), 0)
    return start + jnp.where(row < 8, row - 8, count + row - 8)


def silu_gate(v):
    return 0.5 + 0.5 * jnp.tanh(0.5 * v)


def close_ends(padded, halo, run):
    count = padded.shape[0] - 2 * run
    row = lax.broadcasted_iota(jnp.int32, (run, 1), 0)
    tail = padded[count : count + run, :].astype(F32)
    head = padded[run : 2 * run, :].astype(F32)
    before = jnp.where(row == 0, halo[7:8], pltpu.roll(tail, 1, 0))
    after = jnp.where(row == run - 1, halo[8:9], pltpu.roll(head, run - 1, 0))
    padded[:run, :] = before.astype(BF16)
    padded[run + count :, :] = after.astype(BF16)
    row = lax.broadcasted_iota(jnp.int32, (HALO, 1), 0)
    down = jnp.where(row == 8, tail[run - 1 : run], pltpu.roll(halo, 1, 0))
    up = jnp.where(row == 7, head[:1], pltpu.roll(halo, HALO - 1, 0))
    return [v.astype(BF16) for v in (down, halo, up)]


def taps_product(windows, kernels, layer):
    halves = []
    for half in range(kernels.shape[1]):
        lanes = slice(half * HALF_MXU, (half + 1) * HALF_MXU)
        total = None
        for tap in range(KW):
            term = jnp.dot(
                windows[tap](lanes), kernels[layer, half, tap], preferred_element_type=F32
            )
            total = term if total is None else total + term
        halves.append(total)
    return jnp.concatenate(halves, axis=1)


def forward_kernel(run, devices, chunks, place_ref, *refs):
    received, refs = refs[: chunks * devices], refs[chunks * devices :]
    (stem, kernels, mix, bounds, streams_out, preacts_out, padded_out, feats_out, partial_out,
     streams, preacts, padded, feats, halos, sems) = refs
    layers = mix.shape[0]
    count = 32 * run
    place = place_ref[0]
    start = place * count
    signals = 2 // chunks
    blocks = devices // signals

    row16 = lax.broadcasted_iota(jnp.int32, (HALO, LANES), 0)
    edge = [jnp.zeros((HALO, LANES), F32) for _ in range(2)]
    for chunk in range(chunks):
        for shift in range(devices):
            ref = received[chunk * devices + shift]
            source = (place - shift + devices) % devices
            ends = ref[8 * run :, :].astype(F32)
            channel = chunk if chunks == 2 else source % 2
            lanes = pl.ds(pl.multiple_of(channel * LANES, LANES), LANES)
            for part in range(2):
                block = source // signals
                block = 2 * blocks - 1 - block if part else block
                for c in range(4):
                    at = pl.multiple_of((block + 8 * c) * run, run)
                    feats[pl.ds(at, run), lanes] = ref[
                        (part * 4 + c) * run : (part * 4 + c + 1) * run, :
                    ]
                for which in range(2):
                    value = ends[2 * part + which : 2 * part + which + 1]
                    at = row16 == block + 8 * which
                    for k in range(2):
                        edge[k] = jnp.where(at & (channel == k), value, edge[k])
    for k in range(2):
        feats[count:, k * LANES : (k + 1) * LANES] = edge[k].astype(BF16)
    copies = [pltpu.make_async_copy(feats, feats_out, sems.at[3 * layers])]
    copies[0].start()

    halo_place = halo_column(start, count)
    inside = ((halo_place >= 0) & (halo_place < devices * count)).astype(F32)

    def norm(values):
        scale = lax.rsqrt(jnp.mean(values * values, axis=-1, keepdims=True) + EPS)
        return values * scale

    def stem_tile(i, _):
        at = pl.multiple_of(i * TILE, TILE)
        rows = pl.ds(at, TILE)
        values = jnp.dot(feats[rows, :], stem[...], preferred_element_type=F32)
        streams[0, rows, :] = values
        padded[0, pl.ds(pl.multiple_of(at + run, run), TILE), :] = norm(values).astype(BF16)
        return 0

    lax.fori_loop(0, count // TILE, stem_tile, 0)
    halo_stream = jnp.dot(feats[count:, :], stem[...], preferred_element_type=F32)
    streams[0, count:, :] = halo_stream
    halos[...] = norm(halo_stream) * inside
    partial_out[...] = jnp.zeros_like(partial_out)

    for layer in range(layers):
        here = padded.at[layer]
        windows = close_ends(here, halos[...].astype(BF16).astype(F32), run)
        for k, (src, dst) in enumerate(((streams, streams_out), (padded, padded_out))):
            copy = pltpu.make_async_copy(src.at[layer], dst.at[layer], sems.at[3 * layer + k])
            copy.start()
            copies.append(copy)
        last = layer == layers - 1

        def layer_tile(i, _, layer=layer, here=here, last=last):
            at = pl.multiple_of(i * TILE, TILE)
            rows = pl.ds(at, TILE)
            taps = [
                lambda lanes, t=t: here[pl.ds(pl.multiple_of(at + t * run, run), TILE), lanes]
                for t in range(KW)
            ]
            preact = taps_product(taps, kernels, layer)
            preacts[layer, rows, :] = preact
            active = (preact * silu_gate(preact)).astype(BF16)
            values = streams[layer, rows, :] + jnp.dot(
                active, mix[layer], preferred_element_type=F32
            )
            if last:
                place = position_column(start, run, at, TILE)
                member = (place >= bounds[0:1, :]) & (place < bounds[1:2, :])
                kept = jnp.where(member, values, 0.0)
                partial_out[...] += jnp.sum(kept.reshape(TILE // 8, 8, kept.shape[1]), axis=0)
            else:
                streams[layer + 1, rows, :] = values
                padded[layer + 1, pl.ds(pl.multiple_of(at + run, run), TILE), :] = norm(
                    values
                ).astype(BF16)
            return 0

        lax.fori_loop(0, count // TILE, layer_tile, 0)
        preact = taps_product([lambda lanes, v=v: v[:, lanes] for v in windows], kernels, layer)
        preacts[layer, count:, :] = preact
        if not last:
            active = (preact * silu_gate(preact)).astype(BF16)
            values = streams[layer, count:, :] + jnp.dot(
                active, mix[layer], preferred_element_type=F32
            )
            streams[layer + 1, count:, :] = values
            halos[...] = norm(values) * inside
        copy = pltpu.make_async_copy(
            preacts.at[layer], preacts_out.at[layer], sems.at[3 * layer + 2]
        )
        copy.start()
        copies.append(copy)
    for copy in copies:
        copy.wait()


def backward_kernel(run, devices, all_records, place_ref, *refs):
    sums, refs = refs[:devices], refs[devices:]
    (streams_in, preacts_in, padded_in, feats_in, bounds, head, kernels, mix_t, grads,
     streams, preacts, padded, feats, grad, ahead, active, out16, sems) = refs
    layers = mix_t.shape[0]
    channels = grads.shape[1]
    count = 32 * run
    start = place_ref[0] * count
    order = []
    for layer in reversed(range(layers)):
        for k, (src, dst) in enumerate(
            ((preacts_in, preacts), (padded_in, padded), (streams_in, streams))
        ):
            order.append(pltpu.make_async_copy(src.at[layer], dst.at[layer], sems.at[3 * layer + k]))
    order.append(pltpu.make_async_copy(feats_in, feats, sems.at[3 * layers]))
    for copy in order:
        copy.start()

    total = sums[0][...]
    for ref in sums[1:]:
        total = total + ref[...]
    band_sum = jnp.sum(total, axis=0, keepdims=True)
    counts = (bounds[1:2, :] - bounds[0:1, :]).astype(F32)
    pooled = band_sum / counts
    classes = place_ref[2]
    row = lax.broadcasted_iota(jnp.int32, (HALO, 1), 0)
    logits = jnp.sum(head[...] * pooled, axis=1, keepdims=True)
    exponents = jnp.where(row < classes, jnp.exp(logits), 0.0)
    denominator = jnp.sum(exponents, axis=0, keepdims=True)
    one_hot = (row == place_ref[1]).astype(F32)
    loss = (jnp.log(denominator) - jnp.sum(one_hot * logits, axis=0, keepdims=True)) / all_records
    grad_logits = (exponents / denominator - one_hot) / all_records
    grad_pooled = jnp.sum(head[...] * grad_logits, axis=0, keepdims=True)
    grad_band = grad_pooled / counts
    lead = (place_ref[0] == 0).astype(F32)
    head_at = layers * channels + feats.shape[1] + layers * KW * GROUP_WIDTH
    grads[head_at : head_at + HALO, :] = lead * jnp.where(
        row == HALO - 1, loss, grad_logits * pooled
    )
    if head_at + HALO < grads.shape[0]:
        grads[head_at + HALO :, :] = jnp.zeros_like(grads[head_at + HALO :, :])

    def spread(place):
        member = (place >= bounds[0:1, :]) & (place < bounds[1:2, :])
        return jnp.where(member, grad_band, 0.0)

    def spread_tile(i, _):
        at = pl.multiple_of(i * TILE, TILE)
        grad[pl.ds(at, TILE), :] = spread(position_column(start, run, at, TILE))
        return 0

    lax.fori_loop(0, count // TILE, spread_tile, 0)
    halo_place = halo_column(start, count)
    inside = ((halo_place >= 0) & (halo_place < devices * count)).astype(F32)
    grad[count:, :] = spread(halo_place)

    def gate_grad(preact, grad_act):
        gate = silu_gate(preact)
        return grad_act * gate * (1.0 + preact * (1.0 - gate)), preact * gate

    def stream_grad(grad_out, stream, grad_normed):
        scale = lax.rsqrt(jnp.mean(stream * stream, axis=-1, keepdims=True) + EPS)
        inner = jnp.mean(stream * grad_normed, axis=-1, keepdims=True)
        return grad_out + scale * grad_normed - stream * (scale * scale * scale * inner)

    def transposed(a, b):
        return lax.dot_general(a, b, (((0,), (0,)), ((), ())), preferred_element_type=F32)

    for layer in reversed(range(layers)):
        mine = 3 * (layers - 1 - layer)
        order[mine].wait()
        order[mine + 1].wait()

        def act_tile(i, _, layer=layer):
            at = pl.multiple_of(i * TILE, TILE)
            rows = pl.ds(at, TILE)
            outgoing = grad[rows, :].astype(BF16)
            out16[rows, :] = outgoing
            grad_act = jnp.dot(outgoing, mix_t[layer], preferred_element_type=F32)
            grad_pre, act = gate_grad(preacts[layer, rows, :], grad_act)
            active[rows, :] = act.astype(BF16)
            ahead[pl.ds(pl.multiple_of(at + run, run), TILE), :] = grad_pre.astype(BF16)
            return 0

        lax.fori_loop(0, count // TILE, act_tile, 0)
        grad_act = jnp.dot(grad[count:, :].astype(BF16), mix_t[layer], preferred_element_type=F32)
        halo, _ = gate_grad(preacts[layer, count:, :], grad_act)
        halo = (halo * inside).astype(BF16).astype(F32)
        windows = close_ends(ahead, halo, run)

        def mix_tile(i, _, layer=layer):
            at = pl.multiple_of(i * HALF_MXU, HALF_MXU)
            to = pl.multiple_of(layer * channels + at, HALF_MXU)
            grads[pl.ds(to, HALF_MXU), :] = transposed(
                active[:, pl.ds(at, HALF_MXU)], out16[...]
            )
            return 0

        lax.fori_loop(0, channels // HALF_MXU, mix_tile, 0)

        for half in range(channels // HALF_MXU):
            lanes = slice(half * HALF_MXU, (half + 1) * HALF_MXU)
            at_row = lax.broadcasted_iota(jnp.int32, (HALF_MXU, HALF_MXU), 0) // GROUP_WIDTH
            at_col = lax.broadcasted_iota(jnp.int32, (HALF_MXU, HALF_MXU), 1) // GROUP_WIDTH
            for tap in range(KW):
                full = transposed(
                    padded[layer, tap * run : tap * run + count, lanes],
                    ahead[run : run + count, lanes],
                )
                full = jnp.where(at_row == at_col, full, 0.0)
                folded = jnp.sum(
                    full.reshape(HALF_MXU // GROUP_WIDTH, GROUP_WIDTH, HALF_MXU), axis=0
                )
                to = layers * channels + feats.shape[1] + (layer * KW + tap) * GROUP_WIDTH
                grads[to : to + GROUP_WIDTH, lanes] = folded
        order[mine + 2].wait()

        def stream_tile(i, _, layer=layer):
            at = pl.multiple_of(i * TILE, TILE)
            rows = pl.ds(at, TILE)
            taps = [
                lambda lanes, t=t: ahead[
                    pl.ds(pl.multiple_of(at + (KW - 1 - t) * run, run), TILE), lanes
                ]
                for t in range(KW)
            ]
            grad_normed = taps_product(taps, kernels, layer)
            grad[rows, :] = stream_grad(grad[rows, :], streams[layer, rows, :], grad_normed)
            return 0

        lax.fori_loop(0, count // TILE, stream_tile, 0)
        if layer:
            grad_normed = taps_product(
                [lambda lanes, v=v: v[:, lanes] for v in reversed(windows)], kernels, layer
            )
            grad[count:, :] = stream_grad(
                grad[count:, :], streams[layer, count:, :], grad_normed
            )

    order[-1].wait()

    def split_tile(i, _):
        rows = pl.ds(pl.multiple_of(i * TILE, TILE), TILE)
        values = grad[rows, :]
        high = values.astype(BF16)
        out16[rows, :] = high
        active[rows, :] = (values - high.astype(F32)).astype(BF16)
        return 0

    lax.fori_loop(0, count // TILE, split_tile, 0)
    main = feats[:count, :]
    grads[layers * channels : layers * channels + feats.shape[1], :] = transposed(
        main, out16[...]
    ) + transposed(main, active[...])


def weights_kernel(conv_ref, mix_ref, kernels_ref, turned_ref, mix_t_ref):
    row = lax.broadcasted_iota(jnp.int32, (HALF_MXU, HALF_MXU), 0) // GROUP_WIDTH
    col = lax.broadcasted_iota(jnp.int32, (HALF_MXU, HALF_MXU), 1) // GROUP_WIDTH
    for tap in range(KW):
        for half in range(kernels_ref.shape[0]):
            taps = conv_ref[tap, :, half * HALF_MXU : (half + 1) * HALF_MXU].astype(F32)
            dense = jnp.concatenate([taps] * (HALF_MXU // GROUP_WIDTH), axis=0)
            dense = jnp.where(row == col, dense, 0.0)
            kernels_ref[half, tap] = dense.astype(BF16)
            turned_ref[half, tap] = dense.T.astype(BF16)
    mix_t_ref[...] = mix_ref[...].astype(F32).T.astype(BF16)


def dense_weights(conv_weight, mix_weight):
    layers, taps, width, channels = conv_weight.shape
    dense = (layers, channels // HALF_MXU, taps, HALF_MXU, HALF_MXU)
    by_layer = lambda shape: pl.BlockSpec(
        (None,) + shape[1:], lambda i: (i,) + (0,) * (len(shape) - 1)
    )
    return pl.pallas_call(
        weights_kernel,
        out_shape=[
            jax.ShapeDtypeStruct(dense, BF16),
            jax.ShapeDtypeStruct(dense, BF16),
            jax.ShapeDtypeStruct(mix_weight.shape, BF16),
        ],
        grid=(layers,),
        in_specs=[by_layer(conv_weight.shape), by_layer(mix_weight.shape)],
        out_specs=[by_layer(dense), by_layer(dense), by_layer(mix_weight.shape)],
        compiler_params=pltpu.CompilerParams(vmem_limit_bytes=32 * 1024 * 1024),
        cost_estimate=pl.CostEstimate(flops=0, bytes_accessed=2**24, transcendentals=0),
        name="dense_weights",
    )(conv_weight, mix_weight)


def exchange(x, axis, bit):
    size = lax.axis_size(axis)
    return lax.ppermute(x, axis, [(i, i ^ (1 << bit)) for i in range(size)])


def sum_everywhere(x):
    dp_bits = lax.axis_size("dp").bit_length() - 1
    freq = lax.axis_size("freq")
    place = lax.axis_index("dp")
    for bit in range(dp_bits):
        half = x.shape[0] // 2
        mine = (place >> bit) & 1
        sent = lax.dynamic_slice_in_dim(x, (1 - mine) * half, half, 0)
        kept = lax.dynamic_slice_in_dim(x, mine * half, half, 0)
        x = kept + exchange(sent, "dp", bit)
    part = x.shape[0] // freq
    parts = lax.all_to_all(x.reshape(freq, part, -1), "freq", 0, 0, tiled=True)
    x = jnp.sum(parts, axis=0)
    x = from_all(x, "freq").reshape(freq * part, -1)
    for bit in reversed(range(dp_bits)):
        mine = (place >> bit) & 1
        other = exchange(x, "dp", bit)
        x = jnp.concatenate(
            [jnp.where(mine == 0, x, other), jnp.where(mine == 0, other, x)], axis=0
        )
    return x


def from_all(x, axis):
    size = lax.axis_size(axis)
    pieces = all_of(x, axis)
    stacked = jnp.stack(pieces)
    order = (jnp.arange(size) - lax.axis_index(axis)) % size
    return stacked[(-order) % size]


def shifted(pieces, axis):
    size = len(pieces)
    return [pieces[0]] + [
        lax.ppermute(pieces[k], axis, [(i, (i + k) % size) for i in range(size)])
        for k in range(1, size)
    ]


def all_of(x, axis):
    size = lax.axis_size(axis)
    pieces = [x]
    for shift in range(1, size):
        pieces.append(lax.ppermute(x, axis, [(i, (i + shift) % size) for i in range(size)]))
    return pieces


def local(records, stem_weight, conv_weight, mix_weight, head_weight, labels, band_bounds):
    freq = lax.axis_size("freq")
    place = lax.axis_index("freq").astype(jnp.int32)
    first_len, cols = records.shape[2:]
    second_len = cols * freq
    total_len = first_len * second_len
    layers, channels = mix_weight.shape[:2]
    classes = head_weight.shape[1]
    blocks = first_len // 2 // LANES
    run = second_len // 8 // freq
    count = 32 * run

    section, twiddle = (jnp.asarray(t) for t in first_tables(first_len, second_len))
    spread, table, flip = (jnp.asarray(t) for t in second_tables(second_len))
    here = place.reshape(1)
    signals = freq // blocks
    chunks = 2 // signals
    sent = [
        first_section(here, records[0], c, signals, freq, section, twiddle) for c in range(chunks)
    ]
    arrived = [shifted(pieces, "freq") for pieces in sent]
    features = [
        second_section(here, a, second_len, total_len, spread, table, flip) for a in arrived
    ]
    received = [piece for f in features for piece in shifted(f, "freq")]
    kernels, kernels_t, mix_t = dense_weights(conv_weight, mix_weight)
    head_t = jnp.pad(head_weight.T, ((0, HALO - classes), (0, 0)))
    steps = jnp.repeat(band_bounds // POOL, GROUP_WIDTH)
    bounds = jnp.stack([steps[:channels], steps[GROUP_WIDTH:]]).astype(jnp.int32)

    vmem = pl.BlockSpec(memory_space=pltpu.VMEM)
    hbm = pl.BlockSpec(memory_space=pl.ANY)
    smem = pl.BlockSpec(memory_space=pltpu.SMEM)
    saved = [
        ((layers, count + HALO, channels), F32),
        ((layers, count + HALO, channels), F32),
        ((layers, count + 2 * run, channels), BF16),
        ((count + HALO, 2 * LANES), BF16),
    ]
    *kept, partial = pl.pallas_call(
        functools.partial(forward_kernel, run, freq, chunks),
        out_shape=[jax.ShapeDtypeStruct(s, d) for s, d in saved]
        + [jax.ShapeDtypeStruct((8, channels), F32)],
        in_specs=[smem] + [vmem] * (len(received) + 4),
        out_specs=[hbm] * 4 + [vmem],
        scratch_shapes=[pltpu.VMEM(s, d) for s, d in saved]
        + [pltpu.VMEM((HALO, channels), F32), pltpu.SemaphoreType.DMA((3 * layers + 1,))],
        compiler_params=pltpu.CompilerParams(vmem_limit_bytes=56 * 1024 * 1024),
        name="network_ahead",
    )(here, *received, stem_weight, kernels, mix_weight, bounds)

    sums = all_of(partial, "freq")
    rows = layers * channels + 2 * LANES + layers * KW * GROUP_WIDTH + HALO
    unit_rows = 8 * lax.axis_size("dp") * freq
    rows = -(-rows // unit_rows) * unit_rows
    scalars = jnp.stack([place, labels[0], jnp.int32(classes)])
    grads = pl.pallas_call(
        functools.partial(backward_kernel, run, freq, lax.axis_size("dp")),
        out_shape=jax.ShapeDtypeStruct((rows, channels), F32),
        in_specs=[smem] + [vmem] * freq + [hbm] * 4 + [vmem] * 4,
        out_specs=vmem,
        scratch_shapes=[pltpu.VMEM(s, d) for s, d in saved]
        + [
            pltpu.VMEM((count + HALO, channels), F32),
            pltpu.VMEM((count + 2 * run, channels), BF16),
            pltpu.VMEM((count, channels), BF16),
            pltpu.VMEM((count, channels), BF16),
            pltpu.SemaphoreType.DMA((3 * layers + 1,)),
        ],
        compiler_params=pltpu.CompilerParams(vmem_limit_bytes=60 * 1024 * 1024),
        name="network_back",
    )(scalars, *sums, *kept, bounds, head_t, kernels_t, mix_t)

    total = sum_everywhere(grads)
    mix_rows = layers * channels
    conv_at = mix_rows + 2 * LANES
    head_at = conv_at + layers * KW * GROUP_WIDTH
    return (
        total[head_at + HALO - 1, 0],
        total[mix_rows:conv_at],
        total[conv_at:head_at].reshape(layers, KW, GROUP_WIDTH, channels),
        total[:mix_rows].reshape(layers, channels, channels),
        total[head_at : head_at + classes].T,
    )


def solution(mesh):
    in_specs = (P("dp", None, None, "freq"), P(), P(), P(), P(), P("dp"), P())
    out_specs = (P(), P(), P(), P(), P())
    return jax.shard_map(local, mesh=mesh, in_specs=in_specs, out_specs=out_specs, check_vma=False)
```

time: 949 us -> 294 us (0.31)
  matrix products: 341 us -> 0 us
  waiting for transfers between devices: 292 us -> 88.5 us
  local copies, waits for them, and re-layouts: 120 us -> 15.7 us
  Pallas kernels: 0 us -> 101 us
  blocking collectives: 59.8 us -> 17.3 us
  other arithmetic: 52.3 us -> 12.7 us
  between operations: 17.4 us -> 1.61 us
  loops' own time: 10.6 us -> 0 us
    dot_general x50 -> x0, matrix products: 341 us -> none  [the longest x8 184 us: table_product(): return jnp.einsum('...n,nc->...c', values, table, precision=EXACT_DOTS)]
    all_to_all x3 -> x0, waiting for transfers between devices: 192 us -> none  [the longest x1 182 us: local(): lax.all_to_all(stacked, 'freq', split_axis=3, concat_axis=4, tiled=True)]
    pallas_call x0 -> x7, Pallas kernels: none -> 101 us  [the longest x1 40.9 us: local(): pl.pallas_call(functools.partial(backward_kernel, run, freq, lax.axis_siz...]
    psum x1 -> x0, waiting for transfers between devices: 99.6 us -> none  [local(): lax.psum((loss_part, grad_stem, jnp.stack(conv_grads), jnp.stack(mix_grad...]
    ppermute x12 -> x24, waiting for transfers between devices: 0.03 us -> 88.5 us  [the longest x6 72.4 us: exchange(): return lax.ppermute(x, axis, [(i, i ^ 1 << bit) for i in range(size)])]
    psum x2 -> x0, blocking collectives: 59.8 us -> none  [the longest x1 39.7 us: local(): lax.psum((loss_part, grad_stem, jnp.stack(conv_grads), jnp.stack(mix_grad...]
    dot_general x7 -> x0, local copies, waits for them, and re-layouts: 25.1 us -> none  [the longest x6 24.3 us: conv_weight_grad(): jnp.einsum('rpc,rpd->cd', window, grad_pre, preferred_element_type=jnp.fl...]
    all_to_all x4 -> x0, local copies, waits for them, and re-layouts: 23.8 us -> none  [the longest x2 23 us: local(): lax.all_to_all(stacked, 'freq', split_axis=3, concat_axis=4, tiled=True)]
  transfers between devices with their start and end apart: 16 -> 24, of which waited for: 4 -> 12; matrix products, arithmetic and copies ran while one was open for 10% -> 1% of each run, Pallas kernels for 0% -> 9%
where the time goes in v1:
time: 294 us; the launch traced here: 288 us
  Pallas kernels  101 us (34%)
  waiting for transfers between devices  88.5 us (30%)
  starting transfers between devices  51.6 us (18%)
  blocking collectives  17.3 us (6%)
  local copies, waits for them, and re-layouts  15.7 us (5%)
  other arithmetic  12.7 us (4%)
    ppermute x6, waiting for transfers between devices, exchange(): return lax.ppermute(x, axis, [(i, i ^ 1 << bit) for i in range(size)])  72.4 us
    pallas_call x1, Pallas kernels, local(): pl.pallas_call(functools.partial(backward_kernel, run, freq, lax.axis_siz...  40.9 us
    ppermute x12, starting transfers between devices, shifted(): lax.ppermute(pieces[k], axis, [(i, (i + k) % size) for i in range(size)])  35.5 us
    pallas_call x1, Pallas kernels, local(): pl.pallas_call(functools.partial(forward_kernel, run, freq, chunks), out_...  27 us
    all_to_all x1, blocking collectives, sum_everywhere(): parts = lax.all_to_all(x.reshape(freq, part, -1), 'freq', 0, 0, tiled=True)  17.3 us
    pallas_call x2, Pallas kernels, second_section(): pl.pallas_call(functools.partial(second_kernel, devices, total_len), out_...  16.2 us
    pallas_call x2, Pallas kernels, first_section(): pl.pallas_call(functools.partial(first_kernel, devices), out_shape=[shape...  15.6 us
    ppermute x6, starting transfers between devices, all_of(): lax.ppermute(x, axis, [(i, (i + shift) % size) for i in range(size)])  9.67 us
  transfers between devices with their start and end apart: 24, of which 12 were waited for; matrix products, arithmetic and copies ran while one was open for 1% of the time, Pallas kernels for 9%

profile of v1, /device:TPU:0, one launch (start us, length us, event | category | flops | bytes accessed | tf_op | source)
XLA Modules:
  0.0 288.5 jit_solution(9099514384278587570)
XLA Ops:
  0.6 7.9 %first_section.3 = (s16[544,256]{1,0:T(8,128)(2,1)}, s16[544,256]{1,0:T(8,128)(2,1)}, s16[544,256]{1,0:T(8,128)(2,1)}, s16[544,256]{1,0:T(8,128)(2,1)}) custom-call(s32[1]{0:T(128)} %bitcast.place_ref, f32[2,1024,512]{2,1,0:T(8,128)} %bitcast.18, bf16[2,1024,1024]{2,1,0:T(8,128)(2,1)} %constant.73.clone.table_ref, f32[2048,1024]{1,0:T(8,128)} %constant.74.clone.twiddle_ref), custom_call_target="tpu_custom_call" | custom-call | flops 3221225472 | bytes 8388608 | tf_op jit(solution)/shard_map/first_section/pallas_call | solution.py:105
  8.5 3.0 %collective-permute-start.6 = (s16[544,256]{1,0:T(8,128)(2,1)}, s16[544,256]{1,0:T(8,128)(2,1)S(1)}, u32[]{:S(2)}, u32[]{:S(2)}) collective-permute-start(s16[544,256]{1,0:T(8,128)(2,1)} %get-tuple-element.38), channel_id=1, source_target_pairs={{0,1},{1,2},{2,3},{3,0},{4,5},{5,6},{6,7},{7,4},{8,9},{9,10},{10,1... | collective-permute-start | bytes 835592 | tf_op jit(solution)/shard_map/ppermute | solution.py:613
  11.5 2.6 collective-permute-start.7
  15.5 7.8 %first_section.2 = (s16[544,256]{1,0:T(8,128)(2,1)}, s16[544,256]{1,0:T(8,128)(2,1)}, s16[544,256]{1,0:T(8,128)(2,1)}, s16[544,256]{1,0:T(8,128)(2,1)}) custom-call(s32[1]{0:T(128)} %bitcast.place_ref, f32[2,1024,512]{2,1,0:T(8,128)} %bitcast.19, bf16[2,1024,1024]{2,1,0:T(8,128)(2,1)} %constant.73.clone.table_ref, f32[2048,1024]{1,0:T(8,128)} %constant.74.clone.twiddle_ref), custom_call_target="tpu_custom_call" | custom-call | flops 3221225472 | bytes 8388608 | tf_op jit(solution)/shard_map/first_section/pallas_call | solution.py:105
  24.2 2.9 collective-permute-start.2
  27.1 6.2 %collective-permute-done.7.refs_2_ = s16[544,256]{1,0:T(8,128)(2,1)S(1)} collective-permute-done((s16[544,256]{1,0:T(8,128)(2,1)}, s16[544,256]{1,0:T(8,128)(2,1)S(1)}, u32[]{:S(2)}, u32[]{:S(2)}) %collective-permute-start.7) | collective-permute-done | bytes 278560 | tf_op jit(solution)/shard_map/ppermute | solution.py:613
  36.4 8.1 %second_section.3 = (bf16[528,128]{1,0:T(8,128)(2,1)S(1)}, bf16[528,128]{1,0:T(8,128)(2,1)S(1)}, bf16[528,128]{1,0:T(8,128)(2,1)S(1)}, bf16[528,128]{1,0:T(8,128)(2,1)S(1)}) custom-call(s32[1]{0:T(128)} %bitcast.place_ref, s16[544,256]{1,0:T(8,128)(2,1)S(1)} %copy-done.8, s16[544,256]{1,0:T(8,128)(2,1)S(1)} %collective-permute-done.6.refs_1_, ...), custom_call_target="tpu_custom_call" | custom-call | flops 3221225472 | bytes 8388608 | tf_op jit(solution)/shard_map/second_section/pallas_call | solution.py:209
  45.1 16.7 %collective-permute-start.10 = (bf16[528,128]{1,0:T(8,128)(2,1)S(1)}, bf16[528,128]{1,0:T(8,128)(2,1)S(1)}, u32[]{:S(2)}, u32[]{:S(2)}) collective-permute-start(bf16[528,128]{1,0:T(8,128)(2,1)S(1)} %get-tuple-element.43), channel_id=1, source_target_pairs={{0,2},{1,3},{2,0},{3,1},{4,6},{5,7},{6,4},{7,5},{8,10},{9,11},{10,... | collective-permute-start | bytes 405512 | tf_op jit(solution)/shard_map/ppermute | solution.py:613
  61.8 3.3 %collective-permute-start.11 = (bf16[528,128]{1,0:T(8,128)(2,1)S(1)}, bf16[528,128]{1,0:T(8,128)(2,1)S(1)}, u32[]{:S(2)}, u32[]{:S(2)}) collective-permute-start(bf16[528,128]{1,0:T(8,128)(2,1)S(1)} %get-tuple-element.44), channel_id=1, source_target_pairs={{0,3},{1,0},{2,1},{3,2},{4,7},{5,4},{6,5},{7,6},{8,11},{9,8},{10,9... | collective-permute-start | bytes 405512 | tf_op jit(solution)/shard_map/ppermute | solution.py:613
  65.5 8.1 %second_section.2 = (bf16[528,128]{1,0:T(8,128)(2,1)S(1)}, bf16[528,128]{1,0:T(8,128)(2,1)S(1)}, bf16[528,128]{1,0:T(8,128)(2,1)S(1)}, bf16[528,128]{1,0:T(8,128)(2,1)S(1)}) custom-call(s32[1]{0:T(128)} %bitcast.place_ref, s16[544,256]{1,0:T(8,128)(2,1)S(1)} %copy-done.7, s16[544,256]{1,0:T(8,128)(2,1)S(1)} %collective-permute-done.refs_1_, ...), custom_call_target="tpu_custom_call" | custom-call | flops 3221225472 | bytes 8388608 | tf_op jit(solution)/shard_map/second_section/pallas_call | solution.py:209
  74.2 2.0 collective-permute-start.3
  76.2 2.1 collective-permute-start.4
  87.2 27.0 %network_ahead.1 = (f32[3,2064,512]{2,1,0:T(8,128)}, f32[3,2064,512]{2,1,0:T(8,128)}, bf16[3,2176,512]{2,1,0:T(8,128)(2,1)}, bf16[2064,256]{1,0:T(8,128)(2,1)}, f32[8,512]{1,0:T(8,128)}) custom-call(s32[1]{0:T(128)} %bitcast.place_ref, bf16[528,128]{1,0:T(8,128)(2,1)} %copy-done.6, bf16[528,128]{1,0:T(8,128)(2,1)} %copy-done.16, ...), custom_call_target="tpu_custom_call" | custom-call | tf_op jit(solution)/shard_map/network_ahead/pallas_call | solution.py:665
  114.2 3.4 %collective-permute-start.12 = (f32[8,512]{1,0:T(8,128)}, f32[8,512]{1,0:T(8,128)S(1)}, u32[]{:S(2)}, u32[]{:S(2)}) collective-permute-start(f32[8,512]{1,0:T(8,128)} %get-tuple-element.46.refs_0_), channel_id=1, source_target_pairs={{0,1},{1,2},{2,3},{3,0},{4,5},{5,6},{6,7},{7,4},{8,9},{9,10},{10,1... | collective-permute-start | bytes 49160 | tf_op jit(solution)/shard_map/ppermute | solution.py:622
  123.2 40.9 %network_back.1 = f32[2048,512]{1,0:T(8,128)} custom-call(s32[3]{0:T(128)} %pad_add_fusion.1.place_ref, f32[8,512]{1,0:T(8,128)} %get-tuple-element.46.refs_0_, f32[8,512]{1,0:T(8,128)} %copy-done.20, f32[8,512]{1,0:T(8,128)} %copy-done.21, f32[8,512]{1,0:T(8,128)} %copy-done.22, f32[3,2064,512]{2,1,0:T(8,128)} %get-tuple-element.47.refs_4_, ...), custom_call_target="tpu_custom_call" | custom-call | tf_op jit(solution)/shard_map/network_back/pallas_call | solution.py:682
  164.2 1.8 constant_dynamic-slice_fusion.2
  166.0 4.3 %collective-permute-done.15 = f32[1024,512]{1,0:T(8,128)} collective-permute-done((f32[1024,512]{1,0:T(8,128)S(1)}, f32[1024,512]{1,0:T(8,128)}, u32[]{:S(2)}, u32[]{:S(2)}) %collective-permute-start.15) | collective-permute-done | bytes 2097184 | tf_op jit(solution)/shard_map/ppermute | solution.py:576
  170.3 2.7 dynamic-slice_add_fusion
  174.6 23.8 %collective-permute-done.16 = f32[512,512]{1,0:T(8,128)} collective-permute-done((f32[512,512]{1,0:T(8,128)S(1)}, f32[512,512]{1,0:T(8,128)}, u32[]{:S(2)}, u32[]{:S(2)}) %collective-permute-start.16) | collective-permute-done | bytes 1048608 | tf_op jit(solution)/shard_map/ppermute | solution.py:576
  199.9 1.6 collective-permute-start.17
  201.5 11.6 %collective-permute-done.17 = f32[256,512]{1,0:T(8,128)S(1)} collective-permute-done((f32[256,512]{1,0:T(8,128)S(1)}, f32[256,512]{1,0:T(8,128)S(1)}, u32[]{:S(2)}, u32[]{:S(2)}) %collective-permute-start.17) | collective-permute-done | bytes 524320 | tf_op jit(solution)/shard_map/ppermute | solution.py:576
  213.2 17.3 %all_to_all.5 = f32[4,64,512]{2,1,0:T(8,128)S(1)} all-to-all(f32[4,64,512]{2,1,0:T(8,128)S(1)} %bitcast.22), channel_id=1, replica_groups=mesh['dp'=8,'freq'=4] {'freq'}, dimensions={0} | all-to-all | bytes 1048576 | tf_op jit(solution)/shard_map/all_to_all | solution.py:590
  230.8 1.8 collective-permute-start.19
  232.6 1.8 collective-permute-start.20
  234.4 4.4 %collective-permute-done.18 = f32[64,512]{1,0:T(8,128)S(1)} collective-permute-done((f32[64,512]{1,0:T(8,128)S(1)}, f32[64,512]{1,0:T(8,128)S(1)}, u32[]{:S(2)}, u32[]{:S(2)}) %collective-permute-start.18) | collective-permute-done | bytes 131104 | tf_op jit(solution)/shard_map/ppermute | solution.py:622
  238.8 3.2 %collective-permute-done.19 = f32[64,512]{1,0:T(8,128)S(1)} collective-permute-done((f32[64,512]{1,0:T(8,128)S(1)}, f32[64,512]{1,0:T(8,128)S(1)}, u32[]{:S(2)}, u32[]{:S(2)}) %collective-permute-start.19) | collective-permute-done | bytes 131104 | tf_op jit(solution)/shard_map/ppermute | solution.py:622
  242.7 1.6 collective-permute-start.21
  244.3 8.9 %collective-permute-done.21 = f32[256,512]{1,0:T(8,128)S(1)} collective-permute-done((f32[256,512]{1,0:T(8,128)S(1)}, f32[256,512]{1,0:T(8,128)S(1)}, u32[]{:S(2)}, u32[]{:S(2)}) %collective-permute-start.21) | collective-permute-done | bytes 524320 | tf_op jit(solution)/shard_map/ppermute | solution.py:576
  254.9 19.3 %collective-permute-done.22 = f32[512,512]{1,0:T(8,128)} collective-permute-done((f32[512,512]{1,0:T(8,128)S(1)}, f32[512,512]{1,0:T(8,128)}, u32[]{:S(2)}, u32[]{:S(2)}) %collective-permute-start.22) | collective-permute-done | bytes 1048608 | tf_op jit(solution)/shard_map/ppermute | solution.py:576
  277.2 4.5 %collective-permute-done.23 = f32[1024,512]{1,0:T(8,128)} collective-permute-done((f32[1024,512]{1,0:T(8,128)}, f32[1024,512]{1,0:T(8,128)}, u32[]{:S(2)}, u32[]{:S(2)}) %collective-permute-start.23) | collective-permute-done | bytes 2097184 | tf_op jit(solution)/shard_map/ppermute | solution.py:576
  281.7 2.1 broadcast_select_fusion
  286.5 2.0 pad_maximum_fusion
  (102 shorter events, 32.4 us)
Async XLA Ops:
  8.5 15.8 %collective-permute-start.6 = (s16[544,256]{1,0:T(8,128)(2,1)}, s16[544,256]{1,0:T(8,128)(2,1)S(1)}, u32[]{:S(2)}, u32[]{:S(2)}) collective-permute-start(s16[544,256]{1,0:T(8,128)(2,1)} %get-tuple-element.38), channel_id=1, source_target_pairs={{0,1},{1,2},{2,3},{3,0},{4,5},{5,6},{6,7},{7,4},{8,9},{9,10},{10,1... | collective-permute-start | bytes 835592 | tf_op jit(solution)/shard_map/ppermute | solution.py:613
  11.5 21.8 %collective-permute-start.7 = (s16[544,256]{1,0:T(8,128)(2,1)}, s16[544,256]{1,0:T(8,128)(2,1)S(1)}, u32[]{:S(2)}, u32[]{:S(2)}) collective-permute-start(s16[544,256]{1,0:T(8,128)(2,1)} %get-tuple-element.39), channel_id=1, source_target_pairs={{0,2},{1,3},{2,0},{3,1},{4,6},{5,7},{6,4},{7,5},{8,10},{9,11},{10,... | collective-permute-start | bytes 835592 | tf_op jit(solution)/shard_map/ppermute | solution.py:613
  14.1 10.1 %copy-start.23 = (s32[33]{0:T(128)S(1)}, s32[33]{0:T(128)}, u32[]{:S(2)}) copy-start(s32[33]{0:T(128)} %param.18) | copy-start | bytes 400
  14.1 19.3 %copy-start.8 = (s16[544,256]{1,0:T(8,128)(2,1)S(1)}, s16[544,256]{1,0:T(8,128)(2,1)}, u32[]{:S(2)}) copy-start(s16[544,256]{1,0:T(8,128)(2,1)} %get-tuple-element.37.refs_0_) | copy-start | bytes 835588
  14.1 19.3 %copy-start.12 = (bf16[128,128]{1,0:T(8,128)(2,1)S(1)}, bf16[128,128]{1,0:T(8,128)(2,1)}, u32[]{:S(2)}) copy-start(bf16[128,128]{1,0:T(8,128)(2,1)} %constant.77.clone.refs_6_) | copy-start | bytes 98308
  14.1 19.3 %collective-permute-start.8 = (s16[544,256]{1,0:T(8,128)(2,1)}, s16[544,256]{1,0:T(8,128)(2,1)S(1)}, u32[]{:S(2)}, u32[]{:S(2)}) collective-permute-start(s16[544,256]{1,0:T(8,128)(2,1)} %get-tuple-element.40), channel_id=1, source_target_pairs={{0,3},{1,0},{2,1},{3,2},{4,7},{5,4},{6,5},{7,6},{8,11},{9,8},{10,9... | collective-permute-start | bytes 835592 | tf_op jit(solution)/shard_map/ppermute | solution.py:613
  23.2 41.9 %collective-permute-start = (s16[544,256]{1,0:T(8,128)(2,1)}, s16[544,256]{1,0:T(8,128)(2,1)S(1)}, u32[]{:S(2)}, u32[]{:S(2)}) collective-permute-start(s16[544,256]{1,0:T(8,128)(2,1)} %get-tuple-element.30), channel_id=1, source_target_pairs={{0,1},{1,2},{2,3},{3,0},{4,5},{5,6},{6,7},{7,4},{8,9},{9,10},{10,1... | collective-permute-start | bytes 835592 | tf_op jit(solution)/shard_map/ppermute | solution.py:613
  23.9 41.5 %collective-permute-start.1 = (s16[544,256]{1,0:T(8,128)(2,1)}, s16[544,256]{1,0:T(8,128)(2,1)S(1)}, u32[]{:S(2)}, u32[]{:S(2)}) collective-permute-start(s16[544,256]{1,0:T(8,128)(2,1)} %get-tuple-element.31), channel_id=1, source_target_pairs={{0,2},{1,3},{2,0},{3,1},{4,6},{5,7},{6,4},{7,5},{8,10},{9,11},{10,... | collective-permute-start | bytes 835592 | tf_op jit(solution)/shard_map/ppermute | solution.py:613
  24.2 41.2 %collective-permute-start.2 = (s16[544,256]{1,0:T(8,128)(2,1)}, s16[544,256]{1,0:T(8,128)(2,1)S(1)}, u32[]{:S(2)}, u32[]{:S(2)}) collective-permute-start(s16[544,256]{1,0:T(8,128)(2,1)} %get-tuple-element.32), channel_id=1, source_target_pairs={{0,3},{1,0},{2,1},{3,2},{4,7},{5,4},{6,5},{7,6},{8,11},{9,8},{10,9... | collective-permute-start | bytes 835592 | tf_op jit(solution)/shard_map/ppermute | solution.py:613
  36.4 29.0 %copy-start.7 = (s16[544,256]{1,0:T(8,128)(2,1)S(1)}, s16[544,256]{1,0:T(8,128)(2,1)}, u32[]{:S(2)}) copy-start(s16[544,256]{1,0:T(8,128)(2,1)} %get-tuple-element.29.refs_0_) | copy-start | bytes 835588
  36.4 29.1 %copy-start.10 = (bf16[2,512,1024]{2,1,0:T(8,128)(2,1)S(1)}, bf16[2,512,1024]{2,1,0:T(8,128)(2,1)}, u32[]{:S(2)}) copy-start(bf16[2,512,1024]{2,1,0:T(8,128)(2,1)} %constant.76.clone.refs_5_) | copy-start | bytes 6291460
  45.1 33.2 %collective-permute-start.10 = (bf16[528,128]{1,0:T(8,128)(2,1)S(1)}, bf16[528,128]{1,0:T(8,128)(2,1)S(1)}, u32[]{:S(2)}, u32[]{:S(2)}) collective-permute-start(bf16[528,128]{1,0:T(8,128)(2,1)S(1)} %get-tuple-element.43), channel_id=1, source_target_pairs={{0,2},{1,3},{2,0},{3,1},{4,6},{5,7},{6,4},{7,5},{8,10},{9,11},{10,... | collective-permute-start | bytes 405512 | tf_op jit(solution)/shard_map/ppermute | solution.py:613
  61.8 23.8 %collective-permute-start.11 = (bf16[528,128]{1,0:T(8,128)(2,1)S(1)}, bf16[528,128]{1,0:T(8,128)(2,1)S(1)}, u32[]{:S(2)}, u32[]{:S(2)}) collective-permute-start(bf16[528,128]{1,0:T(8,128)(2,1)S(1)} %get-tuple-element.44), channel_id=1, source_target_pairs={{0,3},{1,0},{2,1},{3,2},{4,7},{5,4},{6,5},{7,6},{8,11},{9,8},{10,9... | collective-permute-start | bytes 405512 | tf_op jit(solution)/shard_map/ppermute | solution.py:613
  65.1 20.5 %collective-permute-start.9 = (bf16[528,128]{1,0:T(8,128)(2,1)S(1)}, bf16[528,128]{1,0:T(8,128)(2,1)S(1)}, u32[]{:S(2)}, u32[]{:S(2)}) collective-permute-start(bf16[528,128]{1,0:T(8,128)(2,1)S(1)} %get-tuple-element.42), channel_id=1, source_target_pairs={{0,1},{1,2},{2,3},{3,0},{4,5},{5,6},{6,7},{7,4},{8,9},{9,10},{10,1... | collective-permute-start | bytes 405512 | tf_op jit(solution)/shard_map/ppermute | solution.py:613
  65.4 14.2 %copy-start = (bf16[3,512,512]{2,1,0:T(8,128)(2,1)S(1)}, bf16[3,512,512]{2,1,0:T(8,128)(2,1)}, u32[]{:S(2)}) copy-start(bf16[3,512,512]{2,1,0:T(8,128)(2,1)} %refs_10_.1) | copy-start | bytes 4718596
  65.4 14.2 %copy-start.4 = (bf16[3,3,16,512]{3,2,1,0:T(8,128)(2,1)S(1)}, bf16[3,3,16,512]{3,2,1,0:T(8,128)(2,1)}, u32[]{:S(2)}) copy-start(bf16[3,3,16,512]{3,2,1,0:T(8,128)(2,1)} %conv_ref.1) | copy-start | bytes 442372
  74.2 11.4 %collective-permute-start.3 = (bf16[528,128]{1,0:T(8,128)(2,1)S(1)}, bf16[528,128]{1,0:T(8,128)(2,1)S(1)}, u32[]{:S(2)}, u32[]{:S(2)}) collective-permute-start(bf16[528,128]{1,0:T(8,128)(2,1)S(1)} %get-tuple-element.34), channel_id=1, source_target_pairs={{0,1},{1,2},{2,3},{3,0},{4,5},{5,6},{6,7},{7,4},{8,9},{9,10},{10,1... | collective-permute-start | bytes 405512 | tf_op jit(solution)/shard_map/ppermute | solution.py:613
  76.2 10.3 %collective-permute-start.4 = (bf16[528,128]{1,0:T(8,128)(2,1)S(1)}, bf16[528,128]{1,0:T(8,128)(2,1)S(1)}, u32[]{:S(2)}, u32[]{:S(2)}) collective-permute-start(bf16[528,128]{1,0:T(8,128)(2,1)S(1)} %get-tuple-element.35), channel_id=1, source_target_pairs={{0,2},{1,3},{2,0},{3,1},{4,6},{5,7},{6,4},{7,5},{8,10},{9,11},{10,... | collective-permute-start | bytes 405512 | tf_op jit(solution)/shard_map/ppermute | solution.py:613
  78.3 8.3 %collective-permute-start.5 = (bf16[528,128]{1,0:T(8,128)(2,1)S(1)}, bf16[528,128]{1,0:T(8,128)(2,1)S(1)}, u32[]{:S(2)}, u32[]{:S(2)}) collective-permute-start(bf16[528,128]{1,0:T(8,128)(2,1)S(1)} %get-tuple-element.36), channel_id=1, source_target_pairs={{0,3},{1,0},{2,1},{3,2},{4,7},{5,4},{6,5},{7,6},{8,11},{9,8},{10,9... | collective-permute-start | bytes 405512 | tf_op jit(solution)/shard_map/ppermute | solution.py:613
  87.2 33.4 %copy-start.19 = (f32[512,10]{0,1:T(8,128)S(1)}, f32[512,10]{0,1:T(8,128)}, u32[]{:S(2)}) copy-start(f32[512,10]{0,1:T(8,128)} %param.16) | copy-start | bytes 61444
  114.2 7.0 %collective-permute-start.12 = (f32[8,512]{1,0:T(8,128)}, f32[8,512]{1,0:T(8,128)S(1)}, u32[]{:S(2)}, u32[]{:S(2)}) collective-permute-start(f32[8,512]{1,0:T(8,128)} %get-tuple-element.46.refs_0_), channel_id=1, source_target_pairs={{0,1},{1,2},{2,3},{3,0},{4,5},{5,6},{6,7},{7,4},{8,9},{9,10},{10,1... | collective-permute-start | bytes 49160 | tf_op jit(solution)/shard_map/ppermute | solution.py:622
  117.6 4.8 %collective-permute-start.13 = (f32[8,512]{1,0:T(8,128)}, f32[8,512]{1,0:T(8,128)S(1)}, u32[]{:S(2)}, u32[]{:S(2)}) collective-permute-start(f32[8,512]{1,0:T(8,128)} %get-tuple-element.46.refs_0_), channel_id=1, source_target_pairs={{0,2},{1,3},{2,0},{3,1},{4,6},{5,7},{6,4},{7,5},{8,10},{9,11},{10,... | collective-permute-start | bytes 49160 | tf_op jit(solution)/shard_map/ppermute | solution.py:622
  118.6 4.0 %collective-permute-start.14 = (f32[8,512]{1,0:T(8,128)}, f32[8,512]{1,0:T(8,128)S(1)}, u32[]{:S(2)}, u32[]{:S(2)}) collective-permute-start(f32[8,512]{1,0:T(8,128)} %get-tuple-element.46.refs_0_), channel_id=1, source_target_pairs={{0,3},{1,0},{2,1},{3,2},{4,7},{5,4},{6,5},{7,6},{8,11},{9,8},{10,9... | collective-permute-start | bytes 49160 | tf_op jit(solution)/shard_map/ppermute | solution.py:622
  165.9 4.4 %collective-permute-start.15 = (f32[1024,512]{1,0:T(8,128)S(1)}, f32[1024,512]{1,0:T(8,128)}, u32[]{:S(2)}, u32[]{:S(2)}) collective-permute-start(f32[1024,512]{1,0:T(8,128)S(1)} %constant_dynamic-slice_fusion.2), channel_id=1, source_target_pairs={{0,4},{4,0},{8,12},{12,8},{16,20},{20,16},{24,28},{28,24},{1,5},{5... | collective-permute-start | bytes 6291464 | tf_op jit(solution)/shard_map/ppermute | solution.py:576
  173.1 25.4 %collective-permute-start.16 = (f32[512,512]{1,0:T(8,128)S(1)}, f32[512,512]{1,0:T(8,128)}, u32[]{:S(2)}, u32[]{:S(2)}) collective-permute-start(f32[512,512]{1,0:T(8,128)S(1)} %constant_dynamic-slice_fusion.1), channel_id=1, source_target_pairs={{0,8},{4,12},{8,0},{12,4},{16,24},{20,28},{24,16},{28,20},{1,9},{5... | collective-permute-start | bytes 3145736 | tf_op jit(solution)/shard_map/ppermute | solution.py:576
  199.9 13.2 %collective-permute-start.17 = (f32[256,512]{1,0:T(8,128)S(1)}, f32[256,512]{1,0:T(8,128)S(1)}, u32[]{:S(2)}, u32[]{:S(2)}) collective-permute-start(f32[256,512]{1,0:T(8,128)S(1)} %constant_dynamic-slice_fusion), channel_id=1, source_target_pairs={{0,16},{4,20},{8,24},{12,28},{16,0},{20,4},{24,8},{28,12},{1,17},{... | collective-permute-start | bytes 1572872 | tf_op jit(solution)/shard_map/ppermute | solution.py:576
  230.5 8.3 %collective-permute-start.18 = (f32[64,512]{1,0:T(8,128)S(1)}, f32[64,512]{1,0:T(8,128)S(1)}, u32[]{:S(2)}, u32[]{:S(2)}) collective-permute-start(f32[64,512]{1,0:T(8,128)S(1)} %reduce_sum.9), channel_id=1, source_target_pairs={{0,1},{1,2},{2,3},{3,0},{4,5},{5,6},{6,7},{7,4},{8,9},{9,10},{10,1... | collective-permute-start | bytes 393224 | tf_op jit(solution)/shard_map/ppermute | solution.py:622
  230.8 11.2 %collective-permute-start.19 = (f32[64,512]{1,0:T(8,128)S(1)}, f32[64,512]{1,0:T(8,128)S(1)}, u32[]{:S(2)}, u32[]{:S(2)}) collective-permute-start(f32[64,512]{1,0:T(8,128)S(1)} %reduce_sum.9), channel_id=1, source_target_pairs={{0,2},{1,3},{2,0},{3,1},{4,6},{5,7},{6,4},{7,5},{8,10},{9,11},{10,... | collective-permute-start | bytes 393224 | tf_op jit(solution)/shard_map/ppermute | solution.py:622
  232.6 9.4 %collective-permute-start.20 = (f32[64,512]{1,0:T(8,128)S(1)}, f32[64,512]{1,0:T(8,128)S(1)}, u32[]{:S(2)}, u32[]{:S(2)}) collective-permute-start(f32[64,512]{1,0:T(8,128)S(1)} %reduce_sum.9), channel_id=1, source_target_pairs={{0,3},{1,0},{2,1},{3,2},{4,7},{5,4},{6,5},{7,6},{8,11},{9,8},{10,9... | collective-permute-start | bytes 393224 | tf_op jit(solution)/shard_map/ppermute | solution.py:622
  242.7 10.5 %collective-permute-start.21 = (f32[256,512]{1,0:T(8,128)S(1)}, f32[256,512]{1,0:T(8,128)S(1)}, u32[]{:S(2)}, u32[]{:S(2)}) collective-permute-start(f32[256,512]{1,0:T(8,128)S(1)} %bitcast.21), channel_id=1, source_target_pairs={{0,16},{4,20},{8,24},{12,28},{16,0},{20,4},{24,8},{28,12},{1,17},{... | collective-permute-start | bytes 1572872 | tf_op jit(solution)/shard_map/ppermute | solution.py:576
  253.4 20.9 %collective-permute-start.22 = (f32[512,512]{1,0:T(8,128)S(1)}, f32[512,512]{1,0:T(8,128)}, u32[]{:S(2)}, u32[]{:S(2)}) collective-permute-start(f32[512,512]{1,0:T(8,128)S(1)} %pad_maximum_fusion.2), channel_id=1, source_target_pairs={{0,8},{4,12},{8,0},{12,4},{16,24},{20,28},{24,16},{28,20},{1,9},{5... | collective-permute-start | bytes 3145736 | tf_op jit(solution)/shard_map/ppermute | solution.py:576
  277.2 4.5 %collective-permute-start.23 = (f32[1024,512]{1,0:T(8,128)}, f32[1024,512]{1,0:T(8,128)}, u32[]{:S(2)}, u32[]{:S(2)}) collective-permute-start(f32[1024,512]{1,0:T(8,128)} %pad_maximum_fusion.1), channel_id=1, source_target_pairs={{0,4},{4,0},{8,12},{12,8},{16,20},{20,16},{24,28},{28,24},{1,5},{5... | collective-permute-start | bytes 6291464 | tf_op jit(solution)/shard_map/ppermute | solution.py:576
  (16 other events, 23.3 us)
